TPU v7x, 512 devices: a whole 4x8x8 slice. The times are simulated.
512 devices in a mesh: dp: 32 (over x, y), seq: 16 (over z, core).
Axes of the slice: x: 4, y: 8, z: 8, core: 2. Of those that a mesh axis runs over, the one named last changes fastest.
Arguments:
- frames: bfloat16 [32, 2048, 1536], P('dp', 'seq'), may hold values from -6 to 6
- lengths: int32 [32], P('dp'), may hold values from 512 to 2048, as said below
- w_qkv: bfloat16 [1536, 16, 288], P(None, 'seq'), may hold values from -1 to 1
- w_out: bfloat16 [16, 96, 1536], P('seq'), may hold values from -0.15625 to 0.15625
- kernel: bfloat16 [9, 1536], replicated, may hold values from -2 to 2
- bn_scale: float32 [1536], replicated, may hold values from 0.5 to 2
- bn_shift: float32 [1536], replicated, may hold values from -3 to 3
- cotangent: bfloat16 [32, 2048, 1536], P('dp', 'seq'), may hold values from -6 to 6
Outputs:
- layer_out: bfloat16 [32, 2048, 1536], P('dp', 'seq')
- grad_qkv: float32 [1536, 16, 288], P('dp', 'seq')
- grad_kernel: float32 [9, 1536], replicated
- grad_scale: float32 [1536], replicated
- grad_shift: float32 [1536], replicated
Inputs may be any that keep to these rules, and one draw needn't show every extreme that they name: `lengths`: some recording has exactly 2048 valid frames in every draw.
All inputs are finite; a program needn't handle non-finite values.
Results may differ from a plain program's by a relative error of at most 0.012.
Values may be sent and summed in bfloat16 or wider, within the bound.
No kernel may reach another device: no remote copies, remote signals or barrier semaphores. Data moves between devices by JAX's collectives and lax.ppermute only.
A program may use at most 64 MiB of HBM per device.

v0:
```python
import jax
import jax.numpy as jnp
from jax import lax
from jax.sharding import PartitionSpec as P

WIN = 128


EPS = 1e-05
FLOOR = 1.0


def padded_2(block, sides, width):
    for axis, dim in sides:
        count = lax.axis_size(axis)
        forward = [(i, i + 1) for i in range(count - 1)]
        backward = [(target, source) for source, target in forward]
        low = lax.ppermute(
            lax.slice_in_dim(block, block.shape[dim] - width, None, axis=dim), axis, forward
        )
        high = lax.ppermute(lax.slice_in_dim(block, 0, width, axis=dim), axis, backward)
        block = jnp.concatenate([low, block, high], axis=dim)
    return block


def layer_norm(rows):
    values = rows.astype(jnp.float32)
    center = values - jnp.mean(values, axis=-1, keepdims=True)
    spread = jnp.mean(center * center, axis=-1, keepdims=True)
    return (center * lax.rsqrt(spread + EPS)).astype(jnp.bfloat16)


def band_keys(key_rows, attention_radius_width):
    segment_count = key_rows.shape[0] // attention_radius_width
    blocks = key_rows.reshape(segment_count, attention_radius_width, key_rows.shape[-1])
    padded = jnp.pad(blocks, ((1, 1), (0, 0), (0, 0)))
    return jnp.concatenate([padded[:-2], padded[1:-1], padded[2:]], axis=1)


def fold_stripe(band, attention_radius_width):
    segment_count = band.shape[0]
    parts = band.reshape(segment_count, 3, attention_radius_width, band.shape[-1])
    padded = jnp.pad(parts, ((1, 1), (0, 0), (0, 0), (0, 0)))
    folded = padded[2:, 0] + padded[1:-1, 1] + padded[:-2, 2]
    return folded.reshape(segment_count * attention_radius_width, band.shape[-1])


def band_mask(segment_count, attention_radius_width, length):
    row_pos = jnp.arange(attention_radius_width, dtype=jnp.int32)[:, None]
    col_pos = jnp.arange(3 * attention_radius_width, dtype=jnp.int32)[None, :]
    nearby = jnp.abs(row_pos + attention_radius_width - col_pos) <= attention_radius_width
    key_pos = (
        jnp.arange(segment_count, dtype=jnp.int32)[:, None, None] * attention_radius_width
        - attention_radius_width
        + col_pos[None]
    )
    return nearby[None] & (key_pos >= 0) & (key_pos < length)


def attend_forward(query_lines, key_rows, value_rows, mask):
    segment_count, attention_radius_width = (mask.shape[0], mask.shape[1])
    query_tiles = query_lines.reshape(segment_count, attention_radius_width, -1)
    neighbour_lookup_rows = band_keys(key_rows, attention_radius_width)
    neighbour_content_rows = band_keys(value_rows, attention_radius_width)
    logit_scores = jnp.einsum(
        "oaz,ofz->oaf", query_tiles, neighbour_lookup_rows, preferred_element_type=jnp.float32
    ) * query_lines.shape[-1] ** (-0.5)
    logit_scores = jnp.where(mask, logit_scores, -1e30)
    top_score = jnp.max(logit_scores, axis=-1, keepdims=True)
    exponent = jnp.where(mask, jnp.exp(logit_scores - top_score), 0.0)
    denominator = jnp.maximum(jnp.sum(exponent, axis=-1, keepdims=True), FLOOR)
    normalized_probabilities = (exponent / denominator).astype(jnp.bfloat16)
    mixed_attention_result = jnp.einsum(
        "mnb,mbo->mno",
        normalized_probabilities,
        neighbour_content_rows,
        preferred_element_type=jnp.float32,
    )
    return (
        mixed_attention_result.reshape(segment_count * attention_radius_width, -1),
        normalized_probabilities,
    )


def attend_backward(query_lines, key_rows, value_rows, normalized_probabilities, grad_rows, mask):
    segment_count, attention_radius_width = (mask.shape[0], mask.shape[1])
    head_dim = query_lines.shape[-1]
    query_tiles = query_lines.reshape(segment_count, attention_radius_width, -1)
    neighbour_lookup_rows = band_keys(key_rows, attention_radius_width)
    neighbour_content_rows = band_keys(value_rows, attention_radius_width)
    block_gradients = grad_rows.reshape(segment_count, attention_radius_width, -1)
    value_gradient = fold_stripe(
        jnp.einsum(
            "ovj,ovp->ojp",
            normalized_probabilities,
            block_gradients,
            preferred_element_type=jnp.float32,
        ),
        attention_radius_width,
    )
    softmax_gradient = jnp.einsum(
        "oaz,ofz->oaf", block_gradients, neighbour_content_rows, preferred_element_type=jnp.float32
    )
    inner = jnp.sum(
        normalized_probabilities.astype(jnp.float32) * softmax_gradient, axis=-1, keepdims=True
    )
    affinity_cotangent = (
        normalized_probabilities.astype(jnp.float32)
        * (softmax_gradient - inner)
        * head_dim ** (-0.5)
    ).astype(jnp.bfloat16)
    request_cotangent = jnp.einsum(
        "mnb,mbo->mno",
        affinity_cotangent,
        neighbour_lookup_rows,
        preferred_element_type=jnp.float32,
    ).reshape(segment_count * attention_radius_width, -1)
    key_gradient = fold_stripe(
        jnp.einsum(
            "ovj,ovp->ojp", affinity_cotangent, query_tiles, preferred_element_type=jnp.float32
        ),
        attention_radius_width,
    )
    return jnp.concatenate([request_cotangent, key_gradient, value_gradient], axis=-1).astype(
        jnp.bfloat16
    )


def on_device(frames, lengths, w_qkv, w_out, kernel, bn_scale, bn_shift, cotangent):
    seq_devices = lax.axis_size("seq")
    local_rows = frames.shape[1]
    model_width = frames.shape[2]
    head_dim = w_out.shape[1]
    seq_total = local_rows * seq_devices
    conv_reach = (kernel.shape[0] - 1) // 2
    length = lengths[0]
    positions = lax.axis_index("seq") * local_rows + jnp.arange(local_rows, dtype=jnp.int32)
    live_here = (positions < length)[:, None]
    live_all = (jnp.arange(seq_total, dtype=jnp.int32) < length)[:, None]
    normed = layer_norm(frames)
    projection = w_qkv.reshape(model_width, 3 * head_dim)
    gathered_rows = lax.all_gather(normed, "seq", axis=1, tiled=True)[0]
    qkv_rows = jnp.dot(gathered_rows, projection, preferred_element_type=jnp.float32).astype(
        jnp.bfloat16
    )
    query_lines = qkv_rows[:, :head_dim]
    key_rows = qkv_rows[:, head_dim : 2 * head_dim]
    value_rows = qkv_rows[:, 2 * head_dim :]
    mask = band_mask(seq_total // WIN, WIN, length)
    mixed_attention_result, normalized_probabilities = attend_forward(
        query_lines, key_rows, value_rows, mask
    )
    head_out = jnp.where(live_all, mixed_attention_result, 0.0).astype(jnp.bfloat16)
    frame_out = lax.all_to_all(
        head_out[None, :, None, :], "seq", split_axis=1, concat_axis=2, tiled=True
    )
    frame_out = frame_out.reshape(local_rows, seq_devices * head_dim)
    out_matrix = lax.all_gather(w_out, "seq", axis=0, tiled=True).reshape(
        seq_devices * head_dim, model_width
    )
    attended = jnp.dot(frame_out, out_matrix, preferred_element_type=jnp.float32)
    hidden = (frames[0].astype(jnp.float32) + attended).astype(jnp.bfloat16)
    masked = jnp.where(live_here, hidden, jnp.zeros_like(hidden))
    padded = padded_2(masked[None], (("seq", 1),), conv_reach)[0].astype(jnp.float32)
    taps = kernel.astype(jnp.float32)
    conv = jnp.zeros((local_rows, model_width), jnp.float32)
    for offset in range(kernel.shape[0]):
        conv = conv + padded[offset : offset + local_rows] * taps[offset]
    shifted = conv * bn_scale + bn_shift
    layer_out = (hidden.astype(jnp.float32) + jax.nn.silu(shifted)).astype(jnp.bfloat16)
    upstream = cotangent[0].astype(jnp.float32)
    sigmoid_val = jax.nn.sigmoid(shifted)
    d_shifted = upstream * sigmoid_val * (1.0 + shifted * (1.0 - sigmoid_val))
    grad_shift = jnp.sum(d_shifted, axis=0)
    grad_scale = jnp.sum(d_shifted * conv, axis=0)
    d_conv = d_shifted * bn_scale
    grad_kernel = jnp.stack(
        [
            jnp.sum(d_conv * padded[offset : offset + local_rows], axis=0)
            for offset in range(kernel.shape[0])
        ]
    )
    d_padded = padded_2(d_conv[None], (("seq", 1),), conv_reach)[0]
    spread = jnp.zeros((local_rows, model_width), jnp.float32)
    for offset in range(kernel.shape[0]):
        spread = (
            spread
            + taps[offset]
            * d_padded[2 * conv_reach - offset : 2 * conv_reach - offset + local_rows]
        )
    d_hidden = (upstream + jnp.where(live_here, spread, 0.0)).astype(jnp.bfloat16)
    d_frame_out = lax.dot_general(
        d_hidden, out_matrix, (((1,), (1,)), ((), ())), preferred_element_type=jnp.float32
    )
    d_frame_out = (
        jnp.where(live_here, d_frame_out, 0.0)
        .astype(jnp.bfloat16)
        .reshape(1, local_rows, seq_devices, head_dim)
    )
    d_head_out = lax.all_to_all(
        d_frame_out, "seq", split_axis=2, concat_axis=1, tiled=True
    ).reshape(seq_total, head_dim)
    d_qkv = attend_backward(
        query_lines, key_rows, value_rows, normalized_probabilities, d_head_out, mask
    )
    grad_local = lax.dot_general(
        gathered_rows, d_qkv, (((0,), (0,)), ((), ())), preferred_element_type=jnp.float32
    )
    grad_local = grad_local.reshape(model_width, 1, 3 * head_dim)
    summed = lax.psum(grad_local, "dp")
    share_rows = model_width // lax.axis_size("dp")
    grad_qkv = lax.dynamic_slice_in_dim(summed, lax.axis_index("dp") * share_rows, share_rows, 0)
    grad_kernel, grad_scale, grad_shift = lax.psum(
        (grad_kernel, grad_scale, grad_shift), ("dp", "seq")
    )
    return (layer_out[None], grad_qkv, grad_kernel, grad_scale, grad_shift)


def solution(mesh):
    in_specs = (
        P("dp", "seq", None),
        P("dp"),
        P(None, "seq", None),
        P("seq", None, None),
        P(),
        P(),
        P(),
        P("dp", "seq", None),
    )
    out_specs = (P("dp", "seq", None), P("dp", "seq", None), P(), P(), P())
    return jax.shard_map(
        on_device, mesh=mesh, in_specs=in_specs, out_specs=out_specs, check_vma=False
    )
```

profile of v0, /device:TPU:1, one launch (start us, length us, event | category | flops | bytes accessed | tf_op | source)
XLA Modules:
  0.0 633.7 jit_solution(15510413581232156315)
XLA Ops:
  7.2 1.2 convert_reduce_fusion
  8.4 1.2 fusion.38
  9.7 2.0 fusion.39
  11.8 0.7 all-gather.5.cloned.1.call-update
  13.2 0.1 abs_compare_fusion
  13.3 53.9 %all-gather.3.cloned.1.call-done = bf16[1,2048,1536]{2,1,0:T(8,128)(2,1)} async-done(((bf16[1,128,1536]{2,1,0:T(8,128)(2,1)}), bf16[1,2048,1536]{2,1,0:T(8,128)(2,1)}) %all-gather.3.cloned.1.call-update) | async-done | bytes 6291472 | tf_op jit(solution)/shard_map/all_gather | solution.py:142
  67.2 4.8 fusion.11
  72.0 0.1 slice_bitcast_fusion.9
  72.2 0.1 copy_bitcast_fusion.5
  72.5 1.1 pad_slice_fusion.13
  73.6 3.5 fusion.113
  77.1 2.3 divide_convert_fusion
  79.4 0.8 fusion.73
  80.2 0.2 copy.55
  80.4 0.2 reshape.301
  80.6 0.8 select_convert_fusion
  81.4 2.3 copy.56
  83.7 0.5 broadcast.223
  84.3 12.3 %reduce.20 = bf16[2048,96]{1,0:T(8,128)(2,1)} reduce(bf16[2048,1,1,96]{3,2,1,0:T(2,128)(2,1)S(1)} %bitcast.192, bf16[]{:T(256)} %broadcast.223), dimensions={1,2}, to_apply=%bitcast.157.reduce_sub_computation | reduce | bytes 786434
  96.6 2.6 reshape.320
  99.2 4.4 all-to-all-start
  103.6 0.2 all-reduce.8.cloned.1.call-start
  103.9 15.3 %all-to-all-done = bf16[16,2,6144]{2,1,0:T(2,128)(2,1)S(1)} async-done(((bf16[16,2,6144]{2,1,0:T(2,128)(2,1)}), bf16[16,2,6144]{2,1,0:T(2,128)(2,1)S(1)}, u32[]{:S(2)}, u32[]{:S(2)}) %all-to-all-start) | async-done | bytes 393248 | tf_op jit(solution)/shard_map/all_to_all | solution.py:154
  119.2 2.0 reshape.321
  121.1 2.3 copy.57
  123.5 0.1 copy.58
  123.7 3.2 fusion.14
  127.0 1.9 collective-permute-start
  128.9 2.4 collective-permute-start.1
  131.3 0.1 slice_reduce_fusion.8
  131.5 2.4 collective-permute-done.1
  134.0 0.1 maximum_convert_fusion
  134.1 2.7 multiply_reduce_fusion.1
  136.8 1.0 fusion.94
  137.8 1.9 collective-permute-start.2
  139.8 3.8 collective-permute-start.3
  143.5 0.9 collective-permute-done.3
  144.5 2.9 fusion.15
  147.4 1.9 copy.59
  149.3 23.9 %all_to_all.30 = bf16[1,128,16,96]{1,3,0,2:T(8,128)(2,1)S(1)} all-to-all(bf16[1,128,16,96]{1,3,0,2:T(8,128)(2,1)} %bitcast.196), channel_id=1, replica_groups=mesh['dp'=32,'seq'=16] {'seq'}, dimensions={2} | all-to-all | bytes 786432 | tf_op jit(solution)/shard_map/all_to_all | solution.py:200
  173.2 3.4 fusion.72
  176.6 4.9 fusion.29
  181.5 5.2 fusion.20
  186.7 1.1 copy.102
  187.8 1.9 copy.99
  189.7 0.1 fusion.66
  189.9 0.2 copy.65
  190.0 0.1 copy.101
  190.2 0.5 convolution_bitcast_fusion
  190.7 0.3 copy.98
  190.9 0.1 fusion.69
  191.1 0.2 copy.68
  191.2 0.1 copy.100
  191.4 1.0 slice-done.2
  192.3 0.8 slice-done.3
  193.2 3.2 fusion.8
  196.6 1.3 stack.39
  197.9 153.8 %all-reduce.8.cloned.1.call-done = f32[1536,1,288]{0,2,1:T(8,128)} async-done(((f32[1536,1,288]{0,2,1:T(8,128)}), f32[1536,1,288]{0,2,1:T(8,128)}) %all-reduce.8.cloned.1.call-update) | async-done | bytes 1769488 | tf_op jit(solution)/shard_map/psum | solution.py:210
  351.8 1.1 constant_dynamic-slice_fusion
  352.8 0.8 copy.69
  353.6 269.5 %all-reduce.10.cloned.1.call-done = (f32[9,1536]{1,0:T(8,128)}, f32[1536]{0:T(1024)}, f32[1536]{0:T(1024)}) async-done(((f32[9,1536]{1,0:T(8,128)}, f32[1536]{0:T(1024)}, f32[1536]{0:T(1024)}), (f32[9,1536]{1,0:T(8,128)}, f32[1536]{0:T(1024)}, f32[1536]{0:T(1024)})) %all-reduce.10.cloned.1.call-update) | async-done | bytes 67600 | tf_op jit(solution)/shard_map/psum | solution.py:213
  623.1 1.5 copy.108
  624.6 1.3 copy.109
  625.9 1.3 copy.110
  (70 shorter events, 0.8 us)
Async XLA Ops:
  7.2 60.1 %copy-start = (bf16[1536,1,288]{0,2,1:T(8,128)(2,1)S(1)}, bf16[1536,1,288]{0,2,1:T(8,128)(2,1)}, u32[]{:S(2)}) copy-start(bf16[1536,1,288]{0,2,1:T(8,128)(2,1)} %param.10) | copy-start | bytes 2654212
  7.2 60.1 %all-gather.3.cloned.1.call-start = ((), (), s32[]{:S(2)}) async-start(), calls=%async_computation.2 | async-start | bytes 6684672 | tf_op jit(solution)/shard_map/all_gather | solution.py:142
  11.7 112.0 %all-gather.5.cloned.1.call-start = ((), (), s32[]{:S(2)}) async-start(), calls=%async_computation.3 | async-start | bytes 5013504 | tf_op jit(solution)/shard_map/all_gather | solution.py:158
  72.2 4.9 copy-start.8
  72.3 4.8 copy-start.6
  72.3 7.1 %copy-start.2 = (bf16[16,128,96]{1,2,0:T(8,128)(2,1)}, bf16[16,128,96]{1,2,0:T(8,128)(2,1)S(1)}, u32[]{:S(2)}) copy-start(bf16[16,128,96]{1,2,0:T(8,128)(2,1)S(1)} %get-tuple-element.67) | copy-start | bytes 1179652
  72.5 4.6 copy-start.10
  72.5 4.6 copy-start.11
  73.6 5.9 copy-start.4
  77.1 2.3 copy-start.5
  81.4 22.5 %copy-start.12 = (bf16[9,1536]{1,0:T(8,128)(2,1)S(1)}, bf16[9,1536]{1,0:T(8,128)(2,1)}, u32[]{:S(2)}) copy-start(bf16[9,1536]{1,0:T(8,128)(2,1)} %param.12) | copy-start | bytes 82948
  99.2 20.0 %all-to-all-start = ((bf16[16,2,6144]{2,1,0:T(2,128)(2,1)}), bf16[16,2,6144]{2,1,0:T(2,128)(2,1)S(1)}, u32[]{:S(2)}, u32[]{:S(2)}) async-start(bf16[16,2,6144]{2,1,0:T(2,128)(2,1)} %reshape.320), calls=%async_computation | async-start | bytes 786432 | tf_op jit(solution)/shard_map/all_to_all | solution.py:154
  103.6 20.0 %copy-start.1 = (bf16[1,128,1536]{2,1,0:T(8,128)(2,1)S(1)}, bf16[1,128,1536]{2,1,0:T(8,128)(2,1)}, u32[]{:S(2)}) copy-start(bf16[1,128,1536]{2,1,0:T(8,128)(2,1)} %param.8) | copy-start | bytes 1179652
  103.6 248.1 %all-reduce.8.cloned.1.call-start = ((), (), s32[]{:S(2)}) async-start(), calls=%async_computation.4 | async-start | bytes 3538944 | tf_op jit(solution)/shard_map/psum | solution.py:210
  123.7 10.4 %copy-start.13 = (f32[1536]{0:T(1024)S(1)}, f32[1536]{0:T(1024)}, u32[]{:S(2)}) copy-start(f32[1536]{0:T(1024)} %param.14) | copy-start | bytes 18436
  123.7 10.4 %copy-start.14 = (f32[1536]{0:T(1024)S(1)}, f32[1536]{0:T(1024)}, u32[]{:S(2)}) copy-start(f32[1536]{0:T(1024)} %param.13) | copy-start | bytes 18436
  126.9 7.2 %copy-start.7 = (bf16[1,128,1536]{2,1,0:T(8,128)(2,1)S(1)}, bf16[1,128,1536]{2,1,0:T(8,128)(2,1)}, u32[]{:S(2)}) copy-start(bf16[1,128,1536]{2,1,0:T(8,128)(2,1)} %param.15) | copy-start | bytes 1179652
  127.0 4.5 collective-permute-start
  128.9 5.0 collective-permute-start.1
  134.1 10.4 %slice-start = ((s8[4718592]{0:T(1024)(128)(4,1)}), s8[4194304]{0:T(1024)(128)(4,1)S(1)}, s32[]{:S(2)}) async-start(s8[4718592]{0:T(1024)(128)(4,1)} %bitcast.189), calls=%async_computation.6 | async-start | bytes 8388608
  134.1 10.4 %slice-start.1 = ((s8[4718592]{0:T(1024)(128)(4,1)}), s8[524288]{0:T(1024)(128)(4,1)S(1)}, s32[]{:S(2)}) async-start(s8[4718592]{0:T(1024)(128)(4,1)} %bitcast.189), calls=%async_computation.7 | async-start | bytes 1048576
  137.8 5.7 collective-permute-start.2
  139.7 33.4 %copy-start.3 = (bf16[16,128,96]{1,2,0:T(8,128)(2,1)S(1)}, bf16[16,128,96]{1,2,0:T(8,128)(2,1)}, u32[]{:S(2)}) copy-start(bf16[16,128,96]{1,2,0:T(8,128)(2,1)} %copy-done.2) | copy-start | bytes 1179652
  139.8 4.7 collective-permute-start.3
  176.6 4.9 copy-start.9
  190.2 2.2 slice-start.2
  190.7 2.5 slice-start.3
  196.4 426.7 %all-reduce.10.cloned.1.call-start = ((), (), s32[]{:S(2)}) async-start(), calls=%async_computation.5 | async-start | bytes 229376 | tf_op jit(solution)/shard_map/psum | solution.py:213
Sparse Core Ops, SparseCore 0:
  11.8 55.3 all-gather.2
  69.4 50.3 all-gather.4
  196.5 155.1 all-reduce.7
  358.6 264.3 all-reduce.9
where the time goes:
time: 635 us; the launch traced here: 634 us
  waiting for transfers between devices  497 us (78%)
  matrix products  32.4 us (5%)
  local copies, waits for them, and re-layouts  26.7 us (4%)
  other arithmetic  24.3 us (4%)
  blocking collectives  23.9 us (4%)
  between operations  15 us (2%)
  starting transfers between devices  14.8 us (2%)
    psum x1, waiting for transfers between devices, on_device(): lax.psum((grad_kernel, grad_scale, grad_shift), ('dp', 'seq'))  269 us
    psum x1, waiting for transfers between devices, on_device(): summed = lax.psum(grad_local, 'dp')  154 us
    all_gather x1, waiting for transfers between devices, on_device(): gathered_rows = lax.all_gather(normed, 'seq', axis=1, tiled=True)[0]  53.9 us
    all_to_all x1, blocking collectives, on_device(): lax.all_to_all(d_frame_out, 'seq', split_axis=2, concat_axis=1, tiled=True)  23.9 us
    all_to_all x1, waiting for transfers between devices, on_device(): lax.all_to_all(head_out[None, :, None, :], 'seq', split_axis=1, concat_ax...  15.3 us
  transfers between devices with their start and end apart: 9, of which 6 were waited for; matrix products, arithmetic and copies ran while one was open for 6% of the time, Pallas kernels for 0%

commit v1 on v0

v1 whole, which is shorter than its diff:
```python
import functools

import jax
import jax.numpy as jnp
from jax import lax
from jax.experimental import pallas as pl
from jax.experimental.pallas import tpu as pltpu
from jax.sharding import PartitionSpec as P

WIN = 128
EPS = 1e-05
FLOOR = 1.0
EDGE = 8
LANES = 128
F32 = jnp.float32
BF16 = jnp.bfloat16

VMEM = pl.BlockSpec(memory_space=pltpu.VMEM)
SMEM = pl.BlockSpec(memory_space=pltpu.SMEM)
ANYWHERE = pl.BlockSpec(memory_space=pl.ANY)


def params(mib):
    return pltpu.CompilerParams(vmem_limit_bytes=mib * 1024 * 1024)


def dot(a, b, dims):
    return lax.dot_general(a, b, ((dims[:1], dims[1:]), ((), ())), preferred_element_type=F32)


def norm_kernel(x_ref, w_ref, packed_ref):
    rows = x_ref.shape[0]
    values = x_ref[...].astype(F32)
    center = values - jnp.mean(values, axis=-1, keepdims=True)
    spread = jnp.mean(center * center, axis=-1, keepdims=True)
    packed_ref[0:rows, :] = (center * lax.rsqrt(spread + EPS)).astype(BF16)
    packed_ref[rows:, :] = w_ref[...]


def forward_kernel(
    len_ref, packed_ref, wt_ref, out_ref, qkvt_ref, k_ref, v_ref, soft_ref, normed, mixed, sems
):
    blocks = packed_ref.shape[0]
    hd = k_ref.shape[1]
    total = blocks * WIN
    per = blocks // sems.shape[0]
    copies = [
        pltpu.make_async_copy(
            packed_ref.at[pl.ds(c * per, per), pl.ds(0, WIN), :],
            normed.at[pl.ds(c * per, per)],
            sems.at[c],
        )
        for c in range(sems.shape[0])
    ]
    for copy in copies:
        copy.start()
    length = len_ref[0]
    for edge in (slice(0, WIN), slice(WIN + total, 2 * WIN + total)):
        qkvt_ref[:, edge] = jnp.zeros((3 * hd, WIN), BF16)
        k_ref[edge, :] = jnp.zeros((WIN, hd), BF16)
        v_ref[edge, :] = jnp.zeros((WIN, hd), BF16)
    mixed[0] = jnp.zeros(mixed.shape[1:], F32)
    mixed[blocks + 1] = jnp.zeros(mixed.shape[1:], F32)
    wt = wt_ref[...]
    for c, copy in enumerate(copies):
        copy.wait()
        rows = normed[c * per : (c + 1) * per].reshape(per * WIN, normed.shape[2])
        part = dot(wt, rows, (1, 1))
        at = slice(WIN + c * per * WIN, WIN + (c + 1) * per * WIN)
        qkvt_ref[:, at] = part.astype(BF16)
        k_ref[at, :] = part[hd : 2 * hd].T.astype(BF16)
        v_ref[at, :] = part[2 * hd :].T.astype(BF16)

    key = lax.broadcasted_iota(jnp.int32, (3 * WIN, WIN), 0)
    query = lax.broadcasted_iota(jnp.int32, (3 * WIN, WIN), 1)
    near = (key >= query) & (key - query <= 2 * WIN)
    column = lax.broadcasted_iota(jnp.int32, (1, WIN), 1)
    scale = hd ** (-0.5)

    def attend(i, carry):
        start = pl.multiple_of(i * WIN, WIN)
        q = qkvt_ref[0:hd, pl.ds(pl.multiple_of(start + WIN, WIN), WIN)]
        key_pos = key + (start - WIN)
        mask = near & (key_pos >= 0) & (key_pos < length)
        scores = dot(k_ref[pl.ds(start, 3 * WIN), :], q, (1, 0)) * scale
        scores = jnp.where(mask, scores, -1e30)
        top = jnp.max(scores, axis=0, keepdims=True)
        expo = jnp.where(mask, jnp.exp(scores - top), 0.0)
        denominator = jnp.maximum(jnp.sum(expo, axis=0, keepdims=True), FLOOR)
        soft = (expo * (1.0 / denominator)).astype(BF16)
        soft_ref[i] = soft
        result = dot(qkvt_ref[2 * hd : 3 * hd, pl.ds(start, 3 * WIN)], soft, (1, 0))
        result = jnp.where(column + start < length, result, 0.0)
        mixed[i + 1, 0:hd, :] = result
        mixed[i + 1, hd:, :] = jnp.zeros((mixed.shape[1] - hd, WIN), F32)
        out_ref[i, 0:hd, :] = result.astype(BF16)
        return carry

    lax.fori_loop(0, blocks, attend, 0, unroll=4)

    def edges(i, carry):
        both = jnp.where(column < EDGE, mixed[i + 2], mixed[i]).T
        rows = jnp.concatenate([both[WIN - EDGE :], both[:EDGE]], axis=0)
        out_ref[i, hd:, :] = rows.astype(BF16)
        return carry

    lax.fori_loop(0, blocks, edges, 0, unroll=4)


def middle_kernel(
    chunk, total, place_ref, mix_ref, packed_ref, x_ref, g_ref, prev_ref, next_ref, taps_ref,
    scale_ref, shift_ref, layer_ref, out_ref, weight, d_hidden, masked, d_conv, small, sem
):
    heads, width = mix_ref.shape[0], x_ref.shape[1]
    rows = x_ref.shape[0]
    hd = weight.shape[1]
    taps_count = taps_ref.shape[0]
    reach = (taps_count - 1) // 2
    ext = rows + 2 * EDGE
    copy = pltpu.make_async_copy(packed_ref.at[:, pl.ds(rows, hd), :], weight, sem)
    copy.start()
    base, length = place_ref[0], place_ref[1]
    body = mix_ref[:, 0:hd, :].reshape(heads * hd, rows).T
    fringe = jnp.concatenate([mix_ref[h, hd:, 0:hd] for h in range(heads)], axis=1)
    mix = jnp.concatenate([body, fringe], axis=0)
    pos = lax.broadcasted_iota(jnp.int32, (ext, 1), 0) + (base - EDGE)
    live = (pos >= 0) & (pos < length)
    inside = (pos >= 0) & (pos < total)
    live_here = live[EDGE : EDGE + rows]
    small[...] = jnp.zeros(small.shape, F32)
    masked[0:reach, :] = jnp.zeros((reach, chunk), F32)
    masked[reach + ext :, :] = jnp.zeros((reach, chunk), F32)
    copy.wait()
    for c in range(width // chunk):
        at = slice(c * chunk, (c + 1) * chunk)
        w = weight[:, :, at].reshape(heads * hd, chunk)
        attended = dot(mix, w, (1, 0))
        attended = jnp.concatenate(
            [attended[rows : rows + EDGE], attended[:rows], attended[rows + EDGE :]], axis=0
        )
        before = prev_ref[:, at].astype(F32)
        after = next_ref[:, at].astype(F32)
        frames = jnp.concatenate([before[:EDGE], x_ref[:, at].astype(F32), after[:EDGE]], axis=0)
        upstream = jnp.concatenate([before[EDGE:], g_ref[:, at].astype(F32), after[EDGE:]], axis=0)
        hidden = (frames + attended).astype(BF16).astype(F32)
        masked[reach : reach + ext, :] = jnp.where(live, hidden, 0.0)
        taps = taps_ref[:, at].astype(F32)
        conv = jnp.zeros((ext, chunk), F32)
        for k in range(taps_count):
            conv = conv + masked[k : k + ext, :] * taps[k : k + 1]
        gain = scale_ref[:, at]
        shifted = conv * gain + shift_ref[:, at]
        sigmoid = jax.nn.sigmoid(shifted)
        d_shifted = upstream * sigmoid * (1.0 + shifted * (1.0 - sigmoid))
        own = slice(EDGE, EDGE + rows)
        layer_ref[:, at] = (hidden[own] + (shifted * sigmoid)[own]).astype(BF16)
        d_own = d_shifted[own]
        small[taps_count : taps_count + 1, at] = jnp.sum(d_own * conv[own], axis=0, keepdims=True)
        small[taps_count + 1 : taps_count + 2, at] = jnp.sum(d_own, axis=0, keepdims=True)
        d_conv[...] = jnp.where(inside, d_shifted * gain, 0.0)
        d_conv_own = d_own * gain
        spread = jnp.zeros((rows, chunk), F32)
        for k in range(taps_count):
            small[k : k + 1, at] = jnp.sum(
                d_conv_own * masked[EDGE + k : EDGE + k + rows, :], axis=0, keepdims=True
            )
            first = EDGE + reach - k
            spread = spread + taps[k : k + 1] * d_conv[first : first + rows, :]
        d_hidden[:, at] = (upstream[own] + jnp.where(live_here, spread, 0.0)).astype(BF16)
    column = lax.broadcasted_iota(jnp.int32, (1, rows), 1) + base
    group = 4
    for h in range(0, heads, group):
        w = weight[h : h + group].reshape(group * hd, width)
        d_mixed = dot(w, d_hidden[...], (1, 1))
        d_mixed = jnp.where(column < length, d_mixed, 0.0).astype(BF16)
        out_ref[h : h + group, 0:hd, :] = d_mixed.reshape(group, hd, rows)
    high = small[...].astype(BF16)
    low = (small[...] - high.astype(F32)).astype(BF16)
    half = small.shape[0]
    for h in range(heads):
        if (h + 1) * LANES <= width:
            at = slice(h * LANES, (h + 1) * LANES)
            out_ref[h, hd : hd + half, :] = high[:, at]
            out_ref[h, hd + half :, :] = low[:, at]
        else:
            out_ref[h, hd:, :] = jnp.zeros((2 * half, rows), BF16)


def backward_kernel(
    shares, in_ref, packed_ref, qkvt_ref, k_ref, v_ref, soft_ref, out_ref,
    normed, d_query, d_key, d_value, joined, grad, sem
):
    blocks, width = packed_ref.shape[0], packed_ref.shape[2]
    hd = k_ref.shape[1]
    total = blocks * WIN
    copy = pltpu.make_async_copy(packed_ref.at[:, pl.ds(0, WIN), :], normed, sem)
    copy.start()
    d_key[...] = jnp.zeros(d_key.shape, F32)
    d_value[...] = jnp.zeros(d_value.shape, F32)
    scale = hd ** (-0.5)

    def attend(i, carry):
        start = pl.multiple_of(i * WIN, WIN)
        own = pl.ds(pl.multiple_of(start + WIN, WIN), WIN)
        window = pl.ds(start, 3 * WIN)
        d_mixed = in_ref[i, 0:hd, :]
        soft = soft_ref[i]
        wide = soft.astype(F32)
        d_soft = dot(v_ref[window, :], d_mixed, (1, 0))
        inner = jnp.sum(wide * d_soft, axis=0, keepdims=True)
        d_scores = (wide * (d_soft - inner) * scale).astype(BF16)
        d_query[:, pl.ds(start, WIN)] = dot(qkvt_ref[hd : 2 * hd, window], d_scores, (1, 0)).astype(BF16)
        d_key[:, window] += dot(qkvt_ref[0:hd, own], d_scores, (1, 1))
        d_value[:, window] += dot(d_mixed, soft, (1, 1))
        return carry

    lax.fori_loop(0, blocks, attend, 0, unroll=4)
    joined[0:hd, :] = d_query[...]
    joined[hd : 2 * hd, :] = d_key[:, WIN : WIN + total].astype(BF16)
    joined[2 * hd :, :] = d_value[:, WIN : WIN + total].astype(BF16)
    copy.wait()
    rest = 3 * hd - 2 * LANES
    copies = LANES // rest
    step = 512
    for c in range(width // step):
        at = slice(c * step, (c + 1) * step)
        rows = normed[:, :, at].reshape(total, step)
        part = dot(joined[...], rows, (1, 0))
        tail = part[2 * LANES :]
        grad[at, :] = jnp.concatenate([part[: 2 * LANES]] + [tail] * copies, axis=0).T
    share = width // shares
    third = share // (copies - 1)
    lane = lax.broadcasted_iota(jnp.int32, (1, LANES), 1) // rest
    half = (in_ref.shape[1] - hd) // 2
    small = jnp.sum(in_ref[:, hd : hd + half, :].astype(F32), axis=0) + jnp.sum(
        in_ref[:, hd + half :, :].astype(F32), axis=0
    )
    small = small.astype(BF16)
    for d in range(shares):
        at = slice(d * share, (d + 1) * share)
        out_ref[d, 0:share, :] = grad[at, 0:LANES].astype(BF16)
        out_ref[d, share : 2 * share, :] = grad[at, LANES : 2 * LANES].astype(BF16)
        packed = jnp.zeros((third, LANES), F32)
        for j in range(copies - 1):
            first = d * share + j * third
            packed = jnp.where(lane == j, grad[first : first + third, 2 * LANES :], packed)
        out_ref[d, 2 * share : 2 * share + third, :] = packed.astype(BF16)
        out_ref[d, 2 * share + third :, :] = small


def sum_kernel(in_ref, grad_ref, small_ref):
    share, columns = grad_ref.shape
    third = in_ref.shape[1] - 2 * share - small_ref.shape[0]
    rest = columns - 2 * LANES
    summed = jnp.sum(in_ref[...].astype(F32), axis=0)
    grad_ref[:, 0:LANES] = summed[0:share]
    grad_ref[:, LANES : 2 * LANES] = summed[share : 2 * share]
    for j in range(share // third):
        grad_ref[j * third : (j + 1) * third, 2 * LANES :] = summed[
            2 * share : 2 * share + third, j * rest : (j + 1) * rest
        ]
    small_ref[...] = summed[2 * share + third :]


def spread_kernel(in_ref, kernel_ref, scale_ref, shift_ref):
    taps = kernel_ref.shape[0]
    for c in range(kernel_ref.shape[1] // LANES):
        at = slice(c * LANES, (c + 1) * LANES)
        kernel_ref[:, at] = in_ref[c, 0:taps, :]
        scale_ref[:, at] = in_ref[c, taps : taps + 1, :]
        shift_ref[:, at] = in_ref[c, taps + 1 : taps + 2, :]


def on_device(frames, lengths, w_qkv, w_out, kernel, bn_scale, bn_shift, cotangent):
    blocks = lax.axis_size("seq")
    shares = lax.axis_size("dp")
    rows, width = frames.shape[1], frames.shape[2]
    hd = w_out.shape[1]
    total = rows * blocks
    taps = kernel.shape[0]
    small_rows = 16
    shape = jax.ShapeDtypeStruct
    x, g = frames[0], cotangent[0]

    with jax.named_scope("norm"):
        packed = pl.pallas_call(
            norm_kernel,
            in_specs=[VMEM, VMEM],
            out_specs=VMEM,
            out_shape=shape((rows + hd, width), BF16),
            compiler_params=params(16),
        )(x, w_out[0])
    with jax.named_scope("gather"):
        gathered = lax.all_gather(packed, "seq")
    with jax.named_scope("halo"):
        upward = [(i, i + 1) for i in range(blocks - 1)]
        downward = [(j, i) for i, j in upward]
        tails = jnp.concatenate([x[rows - EDGE :], g[rows - EDGE :]], axis=0)
        heads = jnp.concatenate([x[:EDGE], g[:EDGE]], axis=0)
        before = lax.ppermute(tails, "seq", upward)
        after = lax.ppermute(heads, "seq", downward)
    wt = w_qkv.reshape(width, 3 * hd).T

    with jax.named_scope("forward"):
        mixed, qkvt, k, v, soft = pl.pallas_call(
            forward_kernel,
            in_specs=[SMEM, ANYWHERE, VMEM],
            out_specs=[VMEM] * 5,
            out_shape=[
                shape((blocks, hd + 2 * EDGE, WIN), BF16),
                shape((3 * hd, total + 2 * WIN), BF16),
                shape((total + 2 * WIN, hd), BF16),
                shape((total + 2 * WIN, hd), BF16),
                shape((blocks, 3 * WIN, WIN), BF16),
            ],
            scratch_shapes=[
                pltpu.VMEM((blocks, WIN, width), BF16),
                pltpu.VMEM((blocks + 2, LANES, WIN), F32),
                pltpu.SemaphoreType.DMA((4,)),
            ],
            compiler_params=params(40),
        )(lengths, gathered, wt)
    with jax.named_scope("mixed_exchange"):
        mixed = lax.all_to_all(mixed, "seq", 0, 0)

    chunk = 256
    with jax.named_scope("middle"):
        place = jnp.stack([lax.axis_index("seq").astype(jnp.int32) * rows, lengths[0]])
        layer_out, d_mixed = pl.pallas_call(
            functools.partial(middle_kernel, chunk, total),
            in_specs=[SMEM, VMEM, ANYWHERE] + [VMEM] * 7,
            out_specs=[VMEM, VMEM],
            out_shape=[
                shape((rows, width), BF16),
                shape((blocks, hd + 2 * small_rows, rows), BF16),
            ],
            scratch_shapes=[
                pltpu.VMEM((blocks, hd, width), BF16),
                pltpu.VMEM((rows, width), BF16),
                pltpu.VMEM((rows + 2 * EDGE + taps - 1, chunk), F32),
                pltpu.VMEM((rows + 2 * EDGE, chunk), F32),
                pltpu.VMEM((small_rows, width), F32),
                pltpu.SemaphoreType.DMA,
            ],
            compiler_params=params(40),
        )(
            place, mixed, gathered, x, g, before, after, kernel,
            bn_scale.reshape(1, width), bn_shift.reshape(1, width),
        )
    with jax.named_scope("d_mixed_exchange"):
        d_mixed = lax.all_to_all(d_mixed, "seq", 0, 0)

    share = width // shares
    third = LANES // 8
    with jax.named_scope("backward"):
        messages = pl.pallas_call(
            functools.partial(backward_kernel, shares),
            in_specs=[VMEM, ANYWHERE] + [VMEM] * 4,
            out_specs=VMEM,
            out_shape=shape((shares, 2 * share + third + small_rows, LANES), BF16),
            scratch_shapes=[
                pltpu.VMEM((blocks, WIN, width), BF16),
                pltpu.VMEM((hd, total), BF16),
                pltpu.VMEM((hd, total + 2 * WIN), F32),
                pltpu.VMEM((hd, total + 2 * WIN), F32),
                pltpu.VMEM((3 * hd, total), BF16),
                pltpu.VMEM((width, 3 * LANES), F32),
                pltpu.SemaphoreType.DMA,
            ],
            compiler_params=params(40),
        )(d_mixed, gathered, qkvt, k, v, soft)
    with jax.named_scope("grad_exchange"):
        messages = lax.all_to_all(messages, "dp", 0, 0)
    with jax.named_scope("sum"):
        grad_qkv, small = pl.pallas_call(
            sum_kernel,
            in_specs=[VMEM],
            out_specs=[VMEM, VMEM],
            out_shape=[shape((share, 3 * hd), F32), shape((small_rows, LANES), F32)],
            compiler_params=params(16),
        )(messages)
    with jax.named_scope("small_gather"):
        small = lax.all_gather(small, "seq")
    with jax.named_scope("spread"):
        grad_kernel, grad_scale, grad_shift = pl.pallas_call(
            spread_kernel,
            in_specs=[VMEM],
            out_specs=[VMEM] * 3,
            out_shape=[shape((taps, width), F32), shape((1, width), F32), shape((1, width), F32)],
            compiler_params=params(16),
        )(small)
    return (
        layer_out[None],
        grad_qkv.reshape(share, 1, 3 * hd),
        grad_kernel,
        grad_scale.reshape(width),
        grad_shift.reshape(width),
    )


def solution(mesh):
    in_specs = (
        P("dp", "seq", None),
        P("dp"),
        P(None, "seq", None),
        P("seq", None, None),
        P(),
        P(),
        P(),
        P("dp", "seq", None),
    )
    out_specs = (P("dp", "seq", None), P("dp", "seq", None), P(), P(), P())
    return jax.shard_map(
        on_device, mesh=mesh, in_specs=in_specs, out_specs=out_specs, check_vma=False
    )
```

time: 635 us -> 223 us (0.35)
  waiting for transfers between devices: 497 us -> 87.4 us
  blocking collectives: 23.9 us -> 72.4 us
  matrix products: 32.4 us -> 0 us
  Pallas kernels: 0 us -> 26.8 us
  other arithmetic: 24.3 us -> 1.32 us
  local copies, waits for them, and re-layouts: 26.7 us -> 10.4 us
    psum x2 -> x0, waiting for transfers between devices: 423 us -> none  [the longest x1 269 us: on_device(): lax.psum((grad_kernel, grad_scale, grad_shift), ('dp', 'seq'))]
    all_to_all x1 -> x2, blocking collectives: 23.9 us -> 57.6 us  [the longest x1 37.2 us: on_device(): messages = lax.all_to_all(messages, 'dp', 0, 0)]
    dot_general x9 -> x0, matrix products: 28.9 us -> none  [the longest x1 5.18 us: attend_backward(): jnp.einsum('ovj,ovp->ojp', affinity_cotangent, query_tiles, preferred_ele...]
    pallas_call x0 -> x6, Pallas kernels: none -> 26.8 us  [the longest x1 10.5 us: on_device(): pl.pallas_call(forward_kernel, in_specs=[SMEM, ANYWHERE, VMEM], out_specs...]
    all_gather x2 -> x1, waiting for transfers between devices: 53.9 us -> 77.1 us  [on_device(): gathered = lax.all_gather(packed, 'seq')]
    all_gather x0 -> x1, blocking collectives: none -> 14.8 us  [on_device(): small = lax.all_gather(small, 'seq')]
    all_to_all x1, waiting for transfers between devices: 15.3 us -> 2.76 us  [on_device(): mixed = lax.all_to_all(mixed, 'seq', 0, 0)]
    unnamed x3 -> x0, other arithmetic: 12.3 us -> none
  transfers between devices with their start and end apart: 9 -> 4, of which waited for: 6 -> 4; matrix products, arithmetic and copies ran while one was open for 6% -> 0% of each run, Pallas kernels for 0% -> 0%
where the time goes in v1:
time: 223 us
  waiting for transfers between devices  87.4 us (39%)
  blocking collectives  72.4 us (32%)
  Pallas kernels  26.8 us (12%)
  between operations  14.8 us (7%)
  local copies, waits for them, and re-layouts  10.4 us (5%)
  starting transfers between devices  9.84 us (4%)
    all_gather x1, waiting for transfers between devices, on_device(): gathered = lax.all_gather(packed, 'seq')  77.1 us
    all_to_all x1, blocking collectives, on_device(): messages = lax.all_to_all(messages, 'dp', 0, 0)  37.2 us
    all_to_all x1, blocking collectives, on_device(): d_mixed = lax.all_to_all(d_mixed, 'seq', 0, 0)  20.5 us
    all_gather x1, blocking collectives, on_device(): small = lax.all_gather(small, 'seq')  14.8 us
    pallas_call x1, Pallas kernels, on_device(): pl.pallas_call(forward_kernel, in_specs=[SMEM, ANYWHERE, VMEM], out_specs...  10.5 us
    unnamed x33, local copies, waits for them, and re-layouts  10.3 us
    pallas_call x1, Pallas kernels, on_device(): pl.pallas_call(functools.partial(backward_kernel, shares), in_specs=[VMEM...  7.81 us
    pallas_call x1, Pallas kernels, on_device(): pl.pallas_call(functools.partial(middle_kernel, chunk, total), in_specs=[...  6.55 us
  transfers between devices with their start and end apart: 4, of which 4 were waited for; matrix products, arithmetic and copies ran while one was open for 0% of the time, Pallas kernels for 0%

profile of v1, /device:TPU:1, one launch (start us, length us, event | category | flops | bytes accessed | tf_op | source)
XLA Modules:
  0.0 223.0 jit_solution(7971460348078055939)
XLA Ops:
  7.2 0.0 all-gather.4.cloned.1.call-start
  7.2 0.0 copy-start.1
  7.2 1.0 copy-done.1
  8.2 0.0 copy-start.12
  8.2 1.0 copy-done.12
  9.2 0.0 copy-start.2
  9.2 0.0 copy-start.5
  9.2 1.1 norm.1
  10.3 0.0 all-gather.4.cloned.1.call-update
  11.0 0.0 copy-done.2
  11.0 77.1 %all-gather.4.cloned.1.call-done = bf16[3584,1536]{1,0:T(8,128)(2,1)} async-done(((bf16[224,1536]{1,0:T(8,128)(2,1)}), bf16[3584,1536]{1,0:T(8,128)(2,1)}) %all-gather.4.cloned.1.call-update) | async-done | bytes 11010064 | tf_op jit(solution)/shard_map/gather/all_gather | solution.py:294
  88.1 0.0 copy-done.5
  88.1 0.0 copy-start.10
  88.1 0.0 copy-start.14
  88.1 0.0 copy-start.15
  88.1 0.0 copy-start.13
  88.1 10.5 %forward.1 = (bf16[16,112,128]{2,1,0:T(8,128)(2,1)S(1)}, bf16[288,2304]{1,0:T(8,128)(2,1)S(1)}, bf16[2304,96]{1,0:T(8,128)(2,1)S(1)}, bf16[2304,96]{1,0:T(8,128)(2,1)S(1)}, bf16[16,384,128]{2,1,0:T(8,128)(2,1)S(1)}) custom-call(s32[1]{0:T(128)S(6)} %copy.14.len_ref, bf16[16,224,1536]{2,1,0:T(8,128)(2,1)} %bitcast.19, bf16[288,1536]{1,0:T(8,128)(2,1)S(1)} %bitcast.24), custom_call_target="tpu_custom_call" | custom-call | tf_op jit(solution)/shard_map/forward/pallas_call | solution.py:305
  98.6 0.0 copy-start.3
  98.6 1.1 copy-done.3
  99.7 0.0 copy-start.6
  99.7 0.8 copy-done.6
  100.5 0.0 copy-start.8
  100.5 0.8 copy-done.8
  101.3 0.0 copy-start.11
  101.3 0.8 copy-done.11
  102.1 4.3 %all-to-all-start = ((bf16[16,112,128]{2,1,0:T(8,128)(2,1)}), bf16[16,112,128]{2,1,0:T(8,128)(2,1)S(1)}, u32[]{:S(2)}, u32[]{:S(2)}) async-start(bf16[16,112,128]{2,1,0:T(8,128)(2,1)} %copy-done.11), calls=%async_computation | async-start | bytes 917504 | tf_op jit(solution)/shard_map/mixed_exchange/all_to_all | solution.py:324
  106.5 0.0 copy-done.10
  106.5 3.5 %collective-permute-start = (bf16[16,1536]{1,0:T(8,128)(2,1)S(1)}, bf16[16,1536]{1,0:T(8,128)(2,1)S(1)}, u32[]{:S(2)}, u32[]{:S(2)}) collective-permute-start(bf16[16,1536]{1,0:T(8,128)(2,1)S(1)} %pad_maximum_fusion), channel_id=1, source_target_pairs={{0,1},{1,2},{2,3},{3,4},{4,5},{5,6},{6,7},{7,8},{8,9},{9,10},{10,1... | collective-permute-start | bytes 147464 | tf_op jit(solution)/shard_map/halo/ppermute | solution.py:300
  110.1 1.9 collective-permute-start.1
  112.0 0.1 pad_add_fusion.place_ref
  112.1 0.0 copy-done.14
  112.1 0.0 copy-done.15
  112.1 4.0 %collective-permute-done.prev_ref = bf16[16,1536]{1,0:T(8,128)(2,1)S(1)} collective-permute-done((bf16[16,1536]{1,0:T(8,128)(2,1)S(1)}, bf16[16,1536]{1,0:T(8,128)(2,1)S(1)}, u32[]{:S(2)}, u32[]{:S(2)}) %collective-permute-start) | collective-permute-done | bytes 49184 | tf_op jit(solution)/shard_map/halo/ppermute | solution.py:300
  116.1 3.6 %collective-permute-done.1.next_ref = bf16[16,1536]{1,0:T(8,128)(2,1)S(1)} collective-permute-done((bf16[16,1536]{1,0:T(8,128)(2,1)S(1)}, bf16[16,1536]{1,0:T(8,128)(2,1)S(1)}, u32[]{:S(2)}, u32[]{:S(2)}) %collective-permute-start.1) | collective-permute-done | bytes 49184 | tf_op jit(solution)/shard_map/halo/ppermute | solution.py:301
  119.7 2.8 %all-to-all-done.mix_ref = bf16[16,112,128]{2,1,0:T(8,128)(2,1)S(1)} async-done(((bf16[16,112,128]{2,1,0:T(8,128)(2,1)}), bf16[16,112,128]{2,1,0:T(8,128)(2,1)S(1)}, u32[]{:S(2)}, u32[]{:S(2)}) %all-to-all-start) | async-done | bytes 458784 | tf_op jit(solution)/shard_map/mixed_exchange/all_to_all | solution.py:324
  122.5 0.0 copy-done.13
  122.5 0.0 copy-start
  122.5 4.1 %copy-done = bf16[3584,1536]{1,0:T(8,128)(2,1)S(1)} copy-done((bf16[3584,1536]{1,0:T(8,128)(2,1)S(1)}, bf16[3584,1536]{1,0:T(8,128)(2,1)}, u32[]{:S(2)}) %copy-start) | copy-done | bytes 11010072
  126.6 0.0 copy-start.4
  126.6 0.0 copy-start.7
  126.6 0.0 copy-start.9
  126.6 6.5 %middle.1 = (bf16[128,1536]{1,0:T(8,128)(2,1)}, bf16[16,128,128]{2,1,0:T(8,128)(2,1)S(1)}) custom-call(s32[2]{0:T(128)S(1)} %pad_add_fusion.place_ref, bf16[16,112,128]{2,1,0:T(8,128)(2,1)S(1)} %all-to-all-done.mix_ref, bf16[16,224,1536]{2,1,0:T(8,128)(2,1)S(1)} %bitcast.21, bf16[128,1536]{1,0:T(8,128)(2,1)S(1)} %bitcast.23, bf16[128,1536]{1,0:T(8,128)(2,1)S(1)} %bitcast.26, ...), custom_call_target="tpu_custom_call" | custom-call | tf_op jit(solution)/shard_map/middle/pallas_call | solution.py:329
  133.1 20.5 %all_to_all.15.in_ref = bf16[16,128,128]{2,1,0:T(8,128)(2,1)S(1)} all-to-all(bf16[16,128,128]{2,1,0:T(8,128)(2,1)S(1)} %get-tuple-element.19), channel_id=1, replica_groups=mesh['dp'=32,'seq'=16] {'seq'}, dimensions={0} | all-to-all | bytes 1048576 | tf_op jit(solution)/shard_map/d_mixed_exchange/all_to_all | solution.py:351
  153.6 0.0 copy-done.4
  153.6 0.0 copy-done.7
  153.6 0.0 copy-done.9
  153.6 7.8 %backward.1 = bf16[32,128,128]{2,1,0:T(8,128)(2,1)S(1)} custom-call(bf16[16,128,128]{2,1,0:T(8,128)(2,1)S(1)} %all_to_all.15.in_ref, bf16[16,224,1536]{2,1,0:T(8,128)(2,1)} %bitcast.20, bf16[288,2304]{1,0:T(8,128)(2,1)S(1)} %copy-done.4, bf16[2304,96]{1,0:T(8,128)(2,1)S(1)} %copy-done.7, bf16[2304,96]{1,0:T(8,128)(2,1)S(1)} %copy-done.9, ...), custom_call_target="tpu_custom_call" | custom-call | tf_op jit(solution)/shard_map/backward/pallas_call | solution.py:356
  161.5 37.2 %all_to_all.16.in_ref = bf16[32,128,128]{2,1,0:T(8,128)(2,1)S(1)} all-to-all(bf16[32,128,128]{2,1,0:T(8,128)(2,1)S(1)} %backward.1), channel_id=1, replica_groups=mesh['dp'=32,'seq'=16] {'dp'}, dimensions={0} | all-to-all | bytes 2097152 | tf_op jit(solution)/shard_map/grad_exchange/all_to_all | solution.py:373
  198.6 0.2 sum.1
  198.8 0.7 copy.13
  199.5 14.8 %all-gather.1 = f32[256,128]{1,0:T(8,128)S(1)} all-gather(f32[16,128]{1,0:T(8,128)S(1)} %get-tuple-element.25), channel_id=3, replica_groups=mesh['dp'=32,'seq'=16] {'seq'}, dimensions={0}, use_global_device_ids=true | all-gather | bytes 139264 | tf_op jit(solution)/shard_map/small_gather/all_gather | solution.py:383
  214.3 0.7 spread.1
  215.0 0.6 reduce
  215.6 0.6 reduce.1
  (6 shorter events, 0.0 us)
Async XLA Ops:
  7.2 80.9 %all-gather.4.cloned.1.call-start = ((), (), s32[]{:S(2)}) async-start(), calls=%async_computation.3 | async-start | bytes 11698176 | tf_op jit(solution)/shard_map/gather/all_gather | solution.py:294
  7.2 1.0 copy-start.1
  8.2 1.0 copy-start.12
  9.2 1.8 copy-start.2
  9.2 78.9 %copy-start.5 = (bf16[1536,1,288]{0,2,1:T(8,128)(2,1)S(1)}, bf16[1536,1,288]{0,2,1:T(8,128)(2,1)}, u32[]{:S(2)}) copy-start(bf16[1536,1,288]{0,2,1:T(8,128)(2,1)} %param.10) | copy-start | bytes 2654212
  88.1 18.4 %copy-start.10 = (bf16[1,128,1536]{2,1,0:T(8,128)(2,1)S(1)}, bf16[1,128,1536]{2,1,0:T(8,128)(2,1)}, u32[]{:S(2)}) copy-start(bf16[1,128,1536]{2,1,0:T(8,128)(2,1)} %param.15) | copy-start | bytes 1179652
  88.1 24.0 %copy-start.14 = (f32[1536]{0:T(1024)S(1)}, f32[1536]{0:T(1024)}, u32[]{:S(2)}) copy-start(f32[1536]{0:T(1024)} %param.13) | copy-start | bytes 18436
  88.1 24.0 %copy-start.15 = (f32[1536]{0:T(1024)S(1)}, f32[1536]{0:T(1024)}, u32[]{:S(2)}) copy-start(f32[1536]{0:T(1024)} %param.14) | copy-start | bytes 18436
  88.1 34.4 %copy-start.13 = (bf16[9,1536]{1,0:T(8,128)(2,1)S(1)}, bf16[9,1536]{1,0:T(8,128)(2,1)}, u32[]{:S(2)}) copy-start(bf16[9,1536]{1,0:T(8,128)(2,1)} %taps_ref.1) | copy-start | bytes 82948
  98.6 1.1 copy-start.3
  99.7 0.8 copy-start.6
  100.5 0.8 copy-start.8
  101.3 0.8 copy-start.11
  102.1 20.3 %all-to-all-start = ((bf16[16,112,128]{2,1,0:T(8,128)(2,1)}), bf16[16,112,128]{2,1,0:T(8,128)(2,1)S(1)}, u32[]{:S(2)}, u32[]{:S(2)}) async-start(bf16[16,112,128]{2,1,0:T(8,128)(2,1)} %copy-done.11), calls=%async_computation | async-start | bytes 917504 | tf_op jit(solution)/shard_map/mixed_exchange/all_to_all | solution.py:324
  106.5 9.6 %collective-permute-start = (bf16[16,1536]{1,0:T(8,128)(2,1)S(1)}, bf16[16,1536]{1,0:T(8,128)(2,1)S(1)}, u32[]{:S(2)}, u32[]{:S(2)}) collective-permute-start(bf16[16,1536]{1,0:T(8,128)(2,1)S(1)} %pad_maximum_fusion), channel_id=1, source_target_pairs={{0,1},{1,2},{2,3},{3,4},{4,5},{5,6},{6,7},{7,8},{8,9},{9,10},{10,1... | collective-permute-start | bytes 147464 | tf_op jit(solution)/shard_map/halo/ppermute | solution.py:300
  110.1 9.6 %collective-permute-start.1 = (bf16[16,1536]{1,0:T(8,128)(2,1)S(1)}, bf16[16,1536]{1,0:T(8,128)(2,1)S(1)}, u32[]{:S(2)}, u32[]{:S(2)}) collective-permute-start(bf16[16,1536]{1,0:T(8,128)(2,1)S(1)} %pad_maximum_fusion.1), channel_id=1, source_target_pairs={{1,0},{2,1},{3,2},{4,3},{5,4},{6,5},{7,6},{8,7},{9,8},{10,9},{11,1... | collective-permute-start | bytes 147464 | tf_op jit(solution)/shard_map/halo/ppermute | solution.py:301
  122.5 4.1 %copy-start = (bf16[3584,1536]{1,0:T(8,128)(2,1)S(1)}, bf16[3584,1536]{1,0:T(8,128)(2,1)}, u32[]{:S(2)}) copy-start(bf16[3584,1536]{1,0:T(8,128)(2,1)} %all-gather.4.cloned.1.call-done) | copy-start | bytes 33030148
  126.6 27.0 %copy-start.4 = (bf16[288,2304]{1,0:T(8,128)(2,1)S(1)}, bf16[288,2304]{1,0:T(8,128)(2,1)}, u32[]{:S(2)}) copy-start(bf16[288,2304]{1,0:T(8,128)(2,1)} %copy-done.3) | copy-start | bytes 3981316
  126.6 27.0 %copy-start.7 = (bf16[2304,96]{1,0:T(8,128)(2,1)S(1)}, bf16[2304,96]{1,0:T(8,128)(2,1)}, u32[]{:S(2)}) copy-start(bf16[2304,96]{1,0:T(8,128)(2,1)} %copy-done.6) | copy-start | bytes 1327108
  126.6 27.0 %copy-start.9 = (bf16[2304,96]{1,0:T(8,128)(2,1)S(1)}, bf16[2304,96]{1,0:T(8,128)(2,1)}, u32[]{:S(2)}) copy-start(bf16[2304,96]{1,0:T(8,128)(2,1)} %copy-done.8) | copy-start | bytes 1327108
Sparse Core Ops, SparseCore 0:
  10.4 77.5 all-gather.3

commit v2 on v1

v2 whole, which is shorter than its diff:
```python
import functools

import jax
import jax.numpy as jnp
from jax import lax
from jax.experimental import pallas as pl
from jax.experimental.pallas import tpu as pltpu
from jax.sharding import PartitionSpec as P

WIN = 128
EPS = 1e-05
FLOOR = 1.0
FAR = -1e30
EDGE = 8
LANES = 128
F32 = jnp.float32
BF16 = jnp.bfloat16

VMEM = pl.BlockSpec(memory_space=pltpu.VMEM)
SMEM = pl.BlockSpec(memory_space=pltpu.SMEM)
HBM = pl.BlockSpec(memory_space=pltpu.HBM)


def params(mib):
    return pltpu.CompilerParams(vmem_limit_bytes=mib * 1024 * 1024)


def dot(a, b, dims):
    return lax.dot_general(a, b, ((dims[:1], dims[1:]), ((), ())), preferred_element_type=F32)


def norm_kernel(x_ref, normed_ref):
    values = x_ref[...].astype(F32)
    center = values - jnp.mean(values, axis=-1, keepdims=True)
    spread = jnp.mean(center * center, axis=-1, keepdims=True)
    normed_ref[...] = (center * lax.rsqrt(spread + EPS)).astype(BF16)


def forward_kernel(
    len_ref, gathered_ref, wt_ref, out_ref, qkvt_out, v_out, soft_out,
    normed, mixed, qkvt_ref, k_ref, v_ref, soft_ref, bias, sems, out_sems
):
    blocks = gathered_ref.shape[0]
    hd = v_ref.shape[1]
    total = blocks * WIN
    per = blocks // sems.shape[0]
    kept = [
        pltpu.make_async_copy(qkvt_ref, qkvt_out, out_sems.at[0]),
        pltpu.make_async_copy(v_ref, v_out, out_sems.at[1]),
    ] + [
        pltpu.make_async_copy(
            soft_ref.at[pl.ds(c * per, per)], soft_out.at[pl.ds(c * per, per)], out_sems.at[2 + c]
        )
        for c in range(sems.shape[0])
    ]
    copies = [
        pltpu.make_async_copy(
            gathered_ref.at[pl.ds(c * per, per)],
            normed.at[pl.ds(c * per, per)],
            sems.at[c],
        )
        for c in range(sems.shape[0])
    ]
    for copy in copies:
        copy.start()
    length = len_ref[0]
    key = lax.broadcasted_iota(jnp.int32, (3 * WIN, WIN), 0)
    query = lax.broadcasted_iota(jnp.int32, (3 * WIN, WIN), 1)
    near = (key >= query) & (key - query <= 2 * WIN)
    bias[...] = jnp.where(near, 0.0, FAR)
    extra = k_ref.shape[1] - hd
    position = lax.broadcasted_iota(jnp.int32, (total + 2 * WIN, extra), 0) - WIN
    dead = (position < 0) | (position >= length)
    k_ref[:, hd:] = jnp.where(dead, FAR, 0.0).astype(BF16)
    ones = (lax.broadcasted_iota(jnp.int32, (extra, WIN), 0) == 0).astype(F32).astype(BF16)
    for edge in (slice(0, WIN), slice(WIN + total, 2 * WIN + total)):
        qkvt_ref[:, edge] = jnp.zeros((3 * hd, WIN), BF16)
        k_ref[edge, 0:hd] = jnp.zeros((WIN, hd), BF16)
        v_ref[edge, :] = jnp.zeros((WIN, hd), BF16)
    mixed[0] = jnp.zeros(mixed.shape[1:], F32)
    mixed[blocks + 1] = jnp.zeros(mixed.shape[1:], F32)
    wt = wt_ref[...]
    for c, copy in enumerate(copies):
        copy.wait()
        rows = normed[c * per : (c + 1) * per].reshape(per * WIN, normed.shape[2])
        part = dot(wt, rows, (1, 1))
        at = slice(WIN + c * per * WIN, WIN + (c + 1) * per * WIN)
        qkvt_ref[:, at] = part.astype(BF16)
        k_ref[at, 0:hd] = part[hd : 2 * hd].T.astype(BF16)
        v_ref[at, :] = part[2 * hd :].T.astype(BF16)

    for copy in kept[:2]:
        copy.start()
    column = lax.broadcasted_iota(jnp.int32, (1, WIN), 1)
    scale = hd ** (-0.5)

    def attend(i, carry):
        start = pl.multiple_of(i * WIN, WIN)
        q = qkvt_ref[0:hd, pl.ds(pl.multiple_of(start + WIN, WIN), WIN)]
        q = jnp.concatenate([q, ones], axis=0)
        scores = dot(k_ref[pl.ds(start, 3 * WIN), :], q, (1, 0)) * scale + bias[...]
        top = jnp.max(scores, axis=0, keepdims=True)
        expo = jnp.exp(scores - top)
        denominator = jnp.maximum(jnp.sum(expo, axis=0, keepdims=True), FLOOR)
        soft = (expo * (1.0 / denominator)).astype(BF16)
        soft_ref[i] = soft
        result = dot(qkvt_ref[2 * hd : 3 * hd, pl.ds(start, 3 * WIN)], soft, (1, 0))
        result = jnp.where(column + start < length, result, 0.0)
        mixed[i + 1, 0:hd, :] = result
        mixed[i + 1, hd:, :] = jnp.zeros((mixed.shape[1] - hd, WIN), F32)
        out_ref[i, 0:hd, :] = result.astype(BF16)
        return carry

    for c in range(sems.shape[0]):
        lax.fori_loop(c * per, (c + 1) * per, attend, 0, unroll=True)
        kept[2 + c].start()

    def edges(i, carry):
        both = jnp.where(column < EDGE, mixed[i + 2], mixed[i]).T
        rows = jnp.concatenate([both[WIN - EDGE :], both[:EDGE]], axis=0)
        out_ref[i, hd:, :] = rows.astype(BF16)
        return carry

    lax.fori_loop(0, blocks, edges, 0, unroll=4)
    for copy in kept:
        copy.wait()


def middle_kernel(
    total, place_ref, mix_in, x_in, g_in, prev_in, next_in, own_ref, near_ref, twin_ref, far_ref,
    twin_far_ref, taps_ref, scale_ref, shift_ref, layer_out, out_ref, mix_ref, x_ref, g_ref,
    prev_ref, next_ref, layer_ref, weight, d_hidden, masked, d_conv, small, sems, more_sems
):
    inputs = [
        pltpu.make_async_copy(source, target, more_sems.at[i])
        for i, (source, target) in enumerate((
            (mix_in, mix_ref), (prev_in, prev_ref), (next_in, next_ref), (x_in, x_ref),
            (g_in, g_ref),
        ))
    ]
    for copy in inputs:
        copy.start()
    heads, width = mix_ref.shape[0], x_ref.shape[1]
    rows = x_ref.shape[0]
    quarters, _, hd, chunk = weight.shape
    core = lax.rem(place_ref[0], 2)
    half = heads // 2
    first, last = pl.ds(0, half), pl.ds(half, half)
    pieces = (
        (0, own_ref.at[first], own_ref.at[last]),
        (2 * core - 1, near_ref.at[first], near_ref.at[last]),
        (1 - 2 * core, twin_ref.at[last], twin_ref.at[first]),
        (2, far_ref, twin_far_ref),
    )

    def fetch(quarter, lower, upper):
        for j, piece in enumerate((lower, upper)):
            target = weight.at[quarter, pl.ds(j * half, half)]
            pltpu.make_async_copy(piece, target, sems.at[quarter, j]).start()

    for quarter in range(quarters):
        for step, lower, upper in pieces:
            holds = lax.rem(place_ref[2] + step + quarters, quarters) == quarter
            pl.when(holds)(functools.partial(fetch, quarter, lower, upper))
    taps_count = taps_ref.shape[0]
    reach = (taps_count - 1) // 2
    ext = rows + 2 * EDGE
    length = place_ref[1]
    base = place_ref[0] * rows
    order = [core + 2 * j for j in range(heads // 2)] + [1 - core + 2 * j for j in range(heads // 2)]
    inputs[0].wait()
    body = jnp.concatenate([mix_ref[h, 0:hd, :] for h in order], axis=0).T
    fringe = jnp.concatenate([mix_ref[h, hd:, 0:hd] for h in order], axis=1)
    mix = jnp.concatenate([body, fringe], axis=0)
    pos = lax.broadcasted_iota(jnp.int32, (ext, 1), 0) + (base - EDGE)
    live = (pos >= 0) & (pos < length)
    inside = (pos >= 0) & (pos < total)
    live_here = live[EDGE : EDGE + rows]
    small[...] = jnp.zeros(small.shape, F32)
    masked[0:reach, :] = jnp.zeros((reach, chunk), F32)
    masked[reach + ext :, :] = jnp.zeros((reach, chunk), F32)
    for copy in inputs[1:]:
        copy.wait()
    for c in range(quarters):
        at = slice(c * chunk, (c + 1) * chunk)
        for j in range(2):
            target = weight.at[c, pl.ds(j * half, half)]
            pltpu.make_async_copy(target, target, sems.at[c, j]).wait()
        w = weight[c].reshape(heads * hd, chunk)
        attended = dot(mix, w, (1, 0))
        attended = jnp.concatenate(
            [attended[rows : rows + EDGE], attended[:rows], attended[rows + EDGE :]], axis=0
        )
        before = prev_ref[:, at].astype(F32)
        after = next_ref[:, at].astype(F32)
        frames = jnp.concatenate([before[:EDGE], x_ref[:, at].astype(F32), after[:EDGE]], axis=0)
        upstream = jnp.concatenate([before[EDGE:], g_ref[:, at].astype(F32), after[EDGE:]], axis=0)
        hidden = (frames + attended).astype(BF16).astype(F32)
        masked[reach : reach + ext, :] = jnp.where(live, hidden, 0.0)
        taps = taps_ref[:, at].astype(F32)
        conv = jnp.zeros((ext, chunk), F32)
        for k in range(taps_count):
            conv = conv + masked[k : k + ext, :] * taps[k : k + 1]
        gain = scale_ref[:, at]
        shifted = conv * gain + shift_ref[:, at]
        sigmoid = jax.nn.sigmoid(shifted)
        d_shifted = upstream * sigmoid * (1.0 + shifted * (1.0 - sigmoid))
        own = slice(EDGE, EDGE + rows)
        layer_ref[:, at] = (hidden[own] + (shifted * sigmoid)[own]).astype(BF16)
        d_own = d_shifted[own]
        small[taps_count : taps_count + 1, at] = jnp.sum(d_own * conv[own], axis=0, keepdims=True)
        small[taps_count + 1 : taps_count + 2, at] = jnp.sum(d_own, axis=0, keepdims=True)
        d_conv[...] = jnp.where(inside, d_shifted * gain, 0.0)
        d_conv_own = d_own * gain
        spread = jnp.zeros((rows, chunk), F32)
        for k in range(taps_count):
            small[k : k + 1, at] = jnp.sum(
                d_conv_own * masked[EDGE + k : EDGE + k + rows, :], axis=0, keepdims=True
            )
            first = EDGE + reach - k
            spread = spread + taps[k : k + 1] * d_conv[first : first + rows, :]
        d_hidden[:, at] = (upstream[own] + jnp.where(live_here, spread, 0.0)).astype(BF16)
    result = pltpu.make_async_copy(layer_ref, layer_out, more_sems.at[len(inputs)])
    result.start()
    column = lax.broadcasted_iota(jnp.int32, (1, rows), 1) + base
    group = 4
    for h in range(0, heads, group):
        d_mixed = jnp.zeros((group * hd, rows), F32)
        for c in range(quarters):
            w = weight[c, h : h + group].reshape(group * hd, chunk)
            d_mixed = d_mixed + dot(w, d_hidden[:, c * chunk : (c + 1) * chunk], (1, 1))
        d_mixed = jnp.where(column < length, d_mixed, 0.0).astype(BF16)
        for j in range(group):
            out_ref[order[h + j], 0:hd, :] = d_mixed[j * hd : (j + 1) * hd]
    high = small[...].astype(BF16)
    low = (small[...] - high.astype(F32)).astype(BF16)
    more = small.shape[0]
    for h in range(heads):
        if (h + 1) * LANES <= width:
            at = slice(h * LANES, (h + 1) * LANES)
            out_ref[h, hd : hd + more, :] = high[:, at]
            out_ref[h, hd + more :, :] = low[:, at]
        else:
            out_ref[h, hd:, :] = jnp.zeros((2 * more, rows), BF16)
    result.wait()


def backward_kernel(
    shares, in_ref, gathered_ref, qkvt_in, v_in, soft_in, out_ref,
    normed, d_query, d_key, d_value, joined, grad, qkvt_ref, v_ref, soft_ref, sems
):
    blocks, width = gathered_ref.shape[0], gathered_ref.shape[2]
    hd = v_ref.shape[1]
    total = blocks * WIN
    groups = sems.shape[0] - 3
    per = blocks // groups
    copies = [
        pltpu.make_async_copy(v_in, v_ref, sems.at[0]),
        pltpu.make_async_copy(qkvt_in, qkvt_ref, sems.at[1]),
    ] + [
        pltpu.make_async_copy(
            soft_in.at[pl.ds(c * per, per)], soft_ref.at[pl.ds(c * per, per)], sems.at[2 + c]
        )
        for c in range(groups)
    ]
    for copy in copies:
        copy.start()
    fetch = pltpu.make_async_copy(gathered_ref, normed, sems.at[2 + groups])
    d_key[...] = jnp.zeros(d_key.shape, F32)
    d_value[...] = jnp.zeros(d_value.shape, F32)
    scale = hd ** (-0.5)

    def attend(i, carry):
        start = pl.multiple_of(i * WIN, WIN)
        own = pl.ds(pl.multiple_of(start + WIN, WIN), WIN)
        window = pl.ds(start, 3 * WIN)
        d_mixed = in_ref[i, 0:hd, :]
        soft = soft_ref[i]
        wide = soft.astype(F32)
        d_soft = dot(v_ref[window, :], d_mixed, (1, 0))
        inner = jnp.sum(wide * d_soft, axis=0, keepdims=True)
        d_scores = (wide * (d_soft - inner) * scale).astype(BF16)
        d_query[:, pl.ds(start, WIN)] = dot(qkvt_ref[hd : 2 * hd, window], d_scores, (1, 0)).astype(BF16)
        d_key[:, window] += dot(qkvt_ref[0:hd, own], d_scores, (1, 1))
        d_value[:, window] += dot(d_mixed, soft, (1, 1))
        return carry

    copies[0].wait()
    copies[1].wait()
    fetch.start()
    for c in range(groups):
        copies[2 + c].wait()
        lax.fori_loop(c * per, (c + 1) * per, attend, 0, unroll=True)
    joined[0:hd, :] = d_query[...]
    joined[hd : 2 * hd, :] = d_key[:, WIN : WIN + total].astype(BF16)
    joined[2 * hd :, :] = d_value[:, WIN : WIN + total].astype(BF16)
    fetch.wait()
    rest = 3 * hd - 2 * LANES
    repeats = LANES // rest
    step = 512
    for c in range(width // step):
        at = slice(c * step, (c + 1) * step)
        rows = normed[:, :, at].reshape(total, step)
        part = dot(joined[...], rows, (1, 0))
        tail = part[2 * LANES :]
        grad[at, :] = jnp.concatenate([part[: 2 * LANES]] + [tail] * repeats, axis=0).T
    share = width // shares
    third = share // (repeats - 1)
    lane = lax.broadcasted_iota(jnp.int32, (1, LANES), 1) // rest
    for d in range(shares):
        at = slice(d * share, (d + 1) * share)
        out_ref[d, 0:share, :] = grad[at, 0:LANES].astype(BF16)
        out_ref[d, share : 2 * share, :] = grad[at, LANES : 2 * LANES].astype(BF16)
        packed = jnp.zeros((third, LANES), F32)
        for j in range(repeats - 1):
            first = d * share + j * third
            packed = jnp.where(lane == j, grad[first : first + third, 2 * LANES :], packed)
        out_ref[d, 2 * share :, :] = packed.astype(BF16)


def sum_kernel(in_ref, grad_ref):
    share, columns = grad_ref.shape[0], grad_ref.shape[2]
    third = in_ref.shape[1] - 2 * share
    rest = columns - 2 * LANES
    summed = jnp.sum(in_ref[...].astype(F32), axis=0)
    grad_ref[:, 0, 0:LANES] = summed[0:share]
    grad_ref[:, 0, LANES : 2 * LANES] = summed[share : 2 * share]
    for j in range(share // third):
        grad_ref[j * third : (j + 1) * third, 0, 2 * LANES :] = summed[
            2 * share : 2 * share + third, j * rest : (j + 1) * rest
        ]


def spread_kernel(in_ref, kernel_ref, scale_ref, shift_ref):
    taps = kernel_ref.shape[0]
    for c in range(kernel_ref.shape[1] // LANES):
        at = slice(c * LANES, (c + 1) * LANES)
        kernel_ref[:, at] = in_ref[c, 0:taps, :]
        scale_ref[at] = in_ref[c, taps, :]
        shift_ref[at] = in_ref[c, taps + 1, :]


def on_device(frames, lengths, w_qkv, w_out, kernel, bn_scale, bn_shift, cotangent):
    blocks = lax.axis_size("seq")
    shares = lax.axis_size("dp")
    rows, width = frames.shape[1], frames.shape[2]
    hd = w_out.shape[1]
    total = rows * blocks
    taps = kernel.shape[0]
    small_rows = 16
    shape = jax.ShapeDtypeStruct
    x, g = frames[0], cotangent[0]

    with jax.named_scope("norm"):
        normed = pl.pallas_call(
            norm_kernel,
            in_specs=[VMEM],
            out_specs=VMEM,
            out_shape=shape((rows, width), BF16),
            compiler_params=params(16),
        )(x)
    with jax.named_scope("gather"):
        gathered = lax.all_gather(normed, "seq")
    with jax.named_scope("halo"):
        upward = [(i, i + 1) for i in range(blocks - 1)]
        downward = [(j, i) for i, j in upward]
        tails = jnp.concatenate([x[rows - EDGE :], g[rows - EDGE :]], axis=0)
        heads = jnp.concatenate([x[:EDGE], g[:EDGE]], axis=0)
        before = lax.ppermute(tails, "seq", upward)
        after = lax.ppermute(heads, "seq", downward)
    firsts = 4
    per = shares // firsts
    chunk = width // firsts
    with jax.named_scope("w_out_columns"):
        quarter = lax.dynamic_slice_in_dim(
            w_out, lax.axis_index("dp") // per * chunk, chunk, axis=2
        )
        same = [list(range(c, blocks, 2)) for c in range(2)]
        twins = [(i, i ^ 1) for i in range(blocks)]
        columns = jnp.broadcast_to(quarter, (blocks // 2, hd, chunk))
        columns = lax.all_to_all(columns, "seq", 0, 0, axis_index_groups=same)
        columns = jnp.concatenate([columns, lax.ppermute(columns, "seq", twins)], axis=0)
        def onward(dp, seq):
            first = (dp // per + 1 - 2 * (seq % 2)) % firsts
            return (first * per + dp % per) * blocks + seq

        ring = [(d * blocks + i, onward(d, i)) for d in range(shares) for i in range(blocks)]
        near = lax.ppermute(columns, ("dp", "seq"), ring)
        near, before, after = lax.optimization_barrier((near, before, after))
        twin = lax.ppermute(near, "seq", twins)
        far = lax.ppermute(near[: blocks // 2], ("dp", "seq"), ring)
        twin_far = lax.ppermute(far, "seq", twins)
    gathered, near = lax.optimization_barrier((gathered, near))
    wt = w_qkv.reshape(width, 3 * hd).T

    with jax.named_scope("forward"):
        mixed, qkvt, v, soft = pl.pallas_call(
            forward_kernel,
            in_specs=[SMEM, HBM, VMEM],
            out_specs=[VMEM] + [HBM] * 3,
            out_shape=[
                shape((blocks, hd + 2 * EDGE, WIN), BF16),
                shape((3 * hd, total + 2 * WIN), BF16),
                shape((total + 2 * WIN, hd), BF16),
                shape((blocks, 3 * WIN, WIN), BF16),
            ],
            scratch_shapes=[
                pltpu.VMEM((blocks, WIN, width), BF16),
                pltpu.VMEM((blocks + 2, LANES, WIN), F32),
                pltpu.VMEM((3 * hd, total + 2 * WIN), BF16),
                pltpu.VMEM((total + 2 * WIN, LANES), BF16),
                pltpu.VMEM((total + 2 * WIN, hd), BF16),
                pltpu.VMEM((blocks, 3 * WIN, WIN), BF16),
                pltpu.VMEM((3 * WIN, WIN), F32),
                pltpu.SemaphoreType.DMA((4,)),
                pltpu.SemaphoreType.DMA((6,)),
            ],
            compiler_params=params(58),
        )(lengths, gathered, wt)
    with jax.named_scope("mixed_exchange"):
        mixed = lax.all_to_all(mixed, "seq", 0, 0)

    with jax.named_scope("middle"):
        place = jnp.stack([lax.axis_index("seq"), lengths[0], lax.axis_index("dp") // per])
        layer_out, d_mixed = pl.pallas_call(
            functools.partial(middle_kernel, total),
            in_specs=[SMEM] + [HBM] * 10 + [VMEM] * 3,
            out_specs=[HBM, VMEM],
            out_shape=[
                shape((rows, width), BF16),
                shape((blocks, hd + 2 * small_rows, rows), BF16),
            ],
            scratch_shapes=[
                pltpu.VMEM(mixed.shape, BF16),
                pltpu.VMEM((rows, width), BF16),
                pltpu.VMEM((rows, width), BF16),
                pltpu.VMEM((2 * EDGE, width), BF16),
                pltpu.VMEM((2 * EDGE, width), BF16),
                pltpu.VMEM((rows, width), BF16),
                pltpu.VMEM((firsts, blocks, hd, chunk), BF16),
                pltpu.VMEM((rows, width), BF16),
                pltpu.VMEM((rows + 2 * EDGE + taps - 1, chunk), F32),
                pltpu.VMEM((rows + 2 * EDGE, chunk), F32),
                pltpu.VMEM((small_rows, width), F32),
                pltpu.SemaphoreType.DMA((firsts, 2)),
                pltpu.SemaphoreType.DMA((6,)),
            ],
            compiler_params=params(60),
        )(
            place, mixed, x, g, before, after, columns, near, twin, far, twin_far, kernel,
            bn_scale.reshape(1, width), bn_shift.reshape(1, width),
        )
    with jax.named_scope("d_mixed_exchange"):
        d_mixed = lax.all_to_all(d_mixed, "seq", 0, 0)

    share = width // shares
    third = LANES // 8
    across = [[i * per + j for i in range(firsts)] for j in range(per)]
    along = [[i * per + j for j in range(per)] for i in range(firsts)]
    with jax.named_scope("small_sums"):
        small = jnp.sum(d_mixed[:, hd:].astype(F32).reshape(2 * blocks, small_rows, LANES), axis=0)
        small = lax.all_to_all(
            jnp.broadcast_to(small, (per,) + small.shape), "dp", 0, 0, axis_index_groups=along
        )
    with jax.named_scope("backward"):
        messages = pl.pallas_call(
            functools.partial(backward_kernel, shares),
            in_specs=[VMEM] + [HBM] * 4,
            out_specs=VMEM,
            out_shape=shape((shares, 2 * share + third, LANES), BF16),
            scratch_shapes=[
                pltpu.VMEM((blocks, WIN, width), BF16),
                pltpu.VMEM((hd, total), BF16),
                pltpu.VMEM((hd, total + 2 * WIN), F32),
                pltpu.VMEM((hd, total + 2 * WIN), F32),
                pltpu.VMEM((3 * hd, total), BF16),
                pltpu.VMEM((width, 3 * LANES), F32),
                pltpu.VMEM((3 * hd, total + 2 * WIN), BF16),
                pltpu.VMEM((total + 2 * WIN, hd), BF16),
                pltpu.VMEM((blocks, 3 * WIN, WIN), BF16),
                pltpu.SemaphoreType.DMA((7,)),
            ],
            compiler_params=params(56),
        )(d_mixed, gathered, qkvt, v, soft)
    messages, small = lax.optimization_barrier((messages, small))
    with jax.named_scope("grad_exchange"):
        messages = lax.all_to_all(messages, "dp", 0, 0)
    with jax.named_scope("small_gathers"):
        small = jnp.sum(small, axis=0)
        small = jnp.sum(lax.all_gather(small, "dp", axis_index_groups=across), axis=0)
        small = lax.all_gather(small, "seq")
    with jax.named_scope("sum"):
        grad_qkv = pl.pallas_call(
            sum_kernel,
            in_specs=[VMEM],
            out_specs=VMEM,
            out_shape=shape((share, 1, 3 * hd), F32),
            compiler_params=params(16),
        )(messages)
    with jax.named_scope("spread"):
        grad_kernel, grad_scale, grad_shift = pl.pallas_call(
            spread_kernel,
            in_specs=[VMEM],
            out_specs=[VMEM] * 3,
            out_shape=[shape((taps, width), F32), shape((width,), F32), shape((width,), F32)],
            compiler_params=params(16),
        )(small)
    return (
        layer_out[None],
        grad_qkv,
        grad_kernel,
        grad_scale,
        grad_shift,
    )


def solution(mesh):
    in_specs = (
        P("dp", "seq", None),
        P("dp"),
        P(None, "seq", None),
        P("seq", None, None),
        P(),
        P(),
        P(),
        P("dp", "seq", None),
    )
    out_specs = (P("dp", "seq", None), P("dp", "seq", None), P(), P(), P())
    return jax.shard_map(
        on_device, mesh=mesh, in_specs=in_specs, out_specs=out_specs, check_vma=False
    )
```

time: 223 us -> 199 us (0.89)
  waiting for transfers between devices: 87.4 us -> 20.8 us
  starting transfers between devices: 9.84 us -> 43.8 us
  Pallas kernels: 26.8 us -> 36.5 us
  local copies, waits for them, and re-layouts: 10.4 us -> 5.61 us
  blocking collectives: 72.4 us -> 75.6 us
    all_gather x1, waiting for transfers between devices: 77.1 us -> 0.02 us  [on_device(): gathered = lax.all_gather(normed, 'seq')]
    ppermute x0 -> x5, starting transfers between devices: none -> 20.1 us  [the longest x1 6.03 us: on_device(): lax.ppermute(columns, 'seq', twins)]
    all_to_all x0 -> x2, starting transfers between devices: none -> 15.5 us  [the longest x1 8.51 us: on_device(): messages = lax.all_to_all(messages, 'dp', 0, 0)]
    all_gather x0 -> x1, blocking collectives: none -> 10.2 us  [on_device(): lax.all_gather(small, 'dp', axis_index_groups=across)]
    all_to_all x1, blocking collectives: 37.2 us -> 28 us  [on_device(): columns = lax.all_to_all(columns, 'seq', 0, 0, axis_index_groups=same)]
    all_to_all x1, waiting for transfers between devices: 2.76 us -> 11.8 us  [on_device(): mixed = lax.all_to_all(mixed, 'seq', 0, 0)]
    unnamed x33 -> x23, local copies, waits for them, and re-layouts: 10.3 us -> 1.9 us
    pallas_call x4, Pallas kernels: 18.3 us -> 24.8 us  [the longest x1 11.8 us: on_device(): pl.pallas_call(forward_kernel, in_specs=[SMEM, HBM, VMEM], out_specs=[VME...]
  transfers between devices with their start and end apart: 4 -> 11, of which waited for: 4 -> 4; matrix products, arithmetic and copies ran while one was open for 0% -> 2% of each run, Pallas kernels for 0% -> 12%
where the time goes in v2:
time: 199 us; the launch traced here: 198 us
  blocking collectives  75.6 us (38%)
  starting transfers between devices  43.8 us (22%)
  Pallas kernels  36.5 us (18%)
  waiting for transfers between devices  20.8 us (10%)
  between operations  15 us (8%)
  local copies, waits for them, and re-layouts  5.61 us (3%)
    all_to_all x1, blocking collectives, on_device(): columns = lax.all_to_all(columns, 'seq', 0, 0, axis_index_groups=same)  28 us
    all_to_all x1, blocking collectives, on_device(): d_mixed = lax.all_to_all(d_mixed, 'seq', 0, 0)  20.1 us
    all_gather x1, blocking collectives, on_device(): small = lax.all_gather(small, 'seq')  17.2 us
    pallas_call x1, Pallas kernels, on_device(): pl.pallas_call(forward_kernel, in_specs=[SMEM, HBM, VMEM], out_specs=[VME...  11.8 us
    all_to_all x1, waiting for transfers between devices, on_device(): mixed = lax.all_to_all(mixed, 'seq', 0, 0)  11.8 us
    pallas_call x1, Pallas kernels, on_device(): pl.pallas_call(functools.partial(middle_kernel, total), in_specs=[SMEM] +...  11.1 us
    pallas_call x1, Pallas kernels, on_device(): pl.pallas_call(functools.partial(backward_kernel, shares), in_specs=[VMEM...  11.1 us
    all_gather x1, blocking collectives, on_device(): lax.all_gather(small, 'dp', axis_index_groups=across)  10.2 us
  transfers between devices with their start and end apart: 11, of which 4 were waited for; matrix products, arithmetic and copies ran while one was open for 2% of the time, Pallas kernels for 12%

profile of v2, /device:TPU:1, one launch (start us, length us, event | category | flops | bytes accessed | tf_op | source)
XLA Modules:
  0.0 198.0 jit_solution(14500556037547501061)
XLA Ops:
  7.2 0.0 copy-start
  7.2 0.0 all-gather.5.cloned.1.call-start
  7.2 0.0 copy-start.1
  7.2 1.0 copy-done.1
  8.3 1.0 norm.1
  9.3 0.0 all-gather.5.cloned.1.call-update
  9.3 0.0 copy-done
  9.4 0.1 broadcast_in_dim.14
  9.4 28.0 %all_to_all.25 = bf16[8,96,384]{2,1,0:T(8,128)(2,1)S(1)} all-to-all(bf16[8,96,384]{2,1,0:T(8,128)(2,1)S(1)} %broadcast_in_dim.14), channel_id=1, replica_groups={{0,2,4,6,8,10,12,14},{1,3,5,7,9,11,13,15},{16,18,20,22,24,26,28,30},{17..., dimensions={0} | all-to-all | bytes 1179648 | tf_op jit(solution)/shard_map/w_out_columns/all_to_all | solution.py:381
  37.5 6.0 %collective-permute-start = (bf16[8,96,384]{2,1,0:T(8,128)(2,1)S(1)}, bf16[8,96,384]{2,1,0:T(8,128)(2,1)S(1)}, u32[]{:S(2)}, u32[]{:S(2)}) collective-permute-start(bf16[8,96,384]{2,1,0:T(8,128)(2,1)S(1)} %all_to_all.25), channel_id=1, source_target_pairs={{0,1},{1,0},{2,3},{3,2},{4,5},{5,4},{6,7},{7,6},{8,9},{9,8},{10,11... | collective-permute-start | bytes 1769480 | tf_op jit(solution)/shard_map/w_out_columns/ppermute | solution.py:382
  43.5 0.1 constant_dynamic-update-slice_fusion.1
  43.6 1.7 collective-permute-done
  45.3 0.1 constant_dynamic-update-slice_fusion.own_ref
  45.4 0.0 copy-start.4
  45.4 4.4 %collective-permute-start.1 = (bf16[16,96,384]{2,1,0:T(8,128)(2,1)S(1)}, bf16[16,96,384]{2,1,0:T(8,128)(2,1)S(1)}, u32[]{:S(2)}, u32[]{:S(2)}) collective-permute-start(bf16[16,96,384]{2,1,0:T(8,128)(2,1)S(1)} %constant_dynamic-update-slice_fusion.own_ref), channel_id=1, source_target_pairs={{0,128},{1,385},{2,130},{3,387},{4,132},{5,389},{6,134},{7,391},{8... | collective-permute-start | bytes 3538952 | tf_op jit(solution)/shard_map/w_out_columns/ppermute | solution.py:388
  49.8 0.8 slice_bitcast_fusion.1
  50.6 0.8 slice_bitcast_fusion
  51.4 1.9 collective-permute-start.2
  53.3 2.4 %collective-permute-start.3 = (bf16[16,1536]{1,0:T(8,128)(2,1)S(1)}, bf16[16,1536]{1,0:T(8,128)(2,1)S(1)}, u32[]{:S(2)}, u32[]{:S(2)}) collective-permute-start(bf16[16,1536]{1,0:T(8,128)(2,1)S(1)} %pad_maximum_fusion.1), channel_id=1, source_target_pairs={{1,0},{2,1},{3,2},{4,3},{5,4},{6,5},{7,6},{8,7},{9,8},{10,9},{11,1... | collective-permute-start | bytes 147464 | tf_op jit(solution)/shard_map/halo/ppermute | solution.py:370
  55.7 0.0 collective-permute-done.2.prev_in
  55.7 0.0 copy-start.7
  55.7 4.0 %collective-permute-done.3.next_in = bf16[16,1536]{1,0:T(8,128)(2,1)S(1)} collective-permute-done((bf16[16,1536]{1,0:T(8,128)(2,1)S(1)}, bf16[16,1536]{1,0:T(8,128)(2,1)S(1)}, u32[]{:S(2)}, u32[]{:S(2)}) %collective-permute-start.3) | collective-permute-done | bytes 49184 | tf_op jit(solution)/shard_map/halo/ppermute | solution.py:370
  59.7 0.0 copy-start.8
  59.7 3.2 %collective-permute-done.1.near_ref = bf16[16,96,384]{2,1,0:T(8,128)(2,1)S(1)} collective-permute-done((bf16[16,96,384]{2,1,0:T(8,128)(2,1)S(1)}, bf16[16,96,384]{2,1,0:T(8,128)(2,1)S(1)}, u32[]{:S(2)}, u32[]{:S(2)}) %collective-permute-start.1) | collective-permute-done | bytes 1179680 | tf_op jit(solution)/shard_map/w_out_columns/ppermute | solution.py:388
  63.0 0.0 copy-start.3
  63.0 0.1 slice.38
  63.0 5.4 %collective-permute-start.5 = (bf16[8,96,384]{2,1,0:T(8,128)(2,1)S(1)}, bf16[8,96,384]{2,1,0:T(8,128)(2,1)}, u32[]{:S(2)}, u32[]{:S(2)}) collective-permute-start(bf16[8,96,384]{2,1,0:T(8,128)(2,1)S(1)} %slice.38), channel_id=1, source_target_pairs={{0,128},{1,385},{2,130},{3,387},{4,132},{5,389},{6,134},{7,391},{8... | collective-permute-start | bytes 1769480 | tf_op jit(solution)/shard_map/w_out_columns/ppermute | solution.py:391
  68.5 1.9 collective-permute-start.4
  71.0 0.0 all-gather.5.cloned.1.call-done
  71.1 0.0 copy-start.9
  71.1 0.0 copy-start.10
  71.1 11.8 %forward.1 = (bf16[16,112,128]{2,1,0:T(8,128)(2,1)}, bf16[288,2304]{1,0:T(8,128)(2,1)}, bf16[2304,96]{1,0:T(8,128)(2,1)}, bf16[16,384,128]{2,1,0:T(8,128)(2,1)}) custom-call(s32[1]{0:T(128)S(6)} %copy.14.len_ref, bf16[16,128,1536]{2,1,0:T(8,128)(2,1)} %bitcast.26, bf16[288,1536]{1,0:T(8,128)(2,1)} %bitcast.28), custom_call_target="tpu_custom_call" | custom-call | tf_op jit(solution)/shard_map/forward/pallas_call | solution.py:397
  82.9 0.0 copy-done.4
  82.9 0.0 copy-done.7
  83.0 0.0 copy-done.8
  83.0 0.0 copy-done.3
  83.0 3.9 %all-to-all-start.1 = ((bf16[16,112,128]{2,1,0:T(8,128)(2,1)}), bf16[16,112,128]{2,1,0:T(8,128)(2,1)S(1)}, u32[]{:S(2)}, u32[]{:S(2)}) async-start(bf16[16,112,128]{2,1,0:T(8,128)(2,1)} %get-tuple-element.23), calls=%async_computation.1 | async-start | bytes 917504 | tf_op jit(solution)/shard_map/mixed_exchange/all_to_all | solution.py:421
  86.8 0.0 collective-permute-done.5.far_ref
  86.8 2.3 %collective-permute-start.6 = (bf16[8,96,384]{2,1,0:T(8,128)(2,1)}, bf16[8,96,384]{2,1,0:T(8,128)(2,1)S(1)}, u32[]{:S(2)}, u32[]{:S(2)}) collective-permute-start(bf16[8,96,384]{2,1,0:T(8,128)(2,1)} %collective-permute-done.5.far_ref), channel_id=1, source_target_pairs={{0,1},{1,0},{2,3},{3,2},{4,5},{5,4},{6,7},{7,6},{8,9},{9,8},{10,11... | collective-permute-start | bytes 1769480 | tf_op jit(solution)/shard_map/w_out_columns/ppermute | solution.py:392
  89.2 0.0 copy-done.9
  89.2 0.6 reshape.30.scale_ref
  89.8 0.0 copy-done.10
  89.8 0.6 reshape.31.shift_ref
  90.4 0.6 pad_add_fusion.place_ref
  91.0 0.0 collective-permute-done.6.twin_far_ref
  91.0 0.0 copy-start.6
  91.0 0.0 collective-permute-done.4.twin_ref
  91.0 11.8 %all-to-all-done.1.mix_in = bf16[16,112,128]{2,1,0:T(8,128)(2,1)S(1)} async-done(((bf16[16,112,128]{2,1,0:T(8,128)(2,1)}), bf16[16,112,128]{2,1,0:T(8,128)(2,1)S(1)}, u32[]{:S(2)}, u32[]{:S(2)}) %all-to-all-start.1) | async-done | bytes 458784 | tf_op jit(solution)/shard_map/mixed_exchange/all_to_all | solution.py:421
  102.8 0.0 copy-start.5
  102.8 0.0 copy-done.6
  102.8 0.8 copy-done.5
  103.6 11.1 %middle.1 = (bf16[128,1536]{1,0:T(8,128)(2,1)}, bf16[16,128,128]{2,1,0:T(8,128)(2,1)}) custom-call(s32[3]{0:T(128)} %pad_add_fusion.place_ref, bf16[16,112,128]{2,1,0:T(8,128)(2,1)} %copy-done.5, bf16[128,1536]{1,0:T(8,128)(2,1)} %bitcast.23, bf16[128,1536]{1,0:T(8,128)(2,1)} %bitcast.30, bf16[16,1536]{1,0:T(8,128)(2,1)} %copy-done.7, ...), custom_call_target="tpu_custom_call" | custom-call | tf_op jit(solution)/shard_map/middle/pallas_call | solution.py:425
  114.7 20.1 %all_to_all.26.in_ref = bf16[16,128,128]{2,1,0:T(8,128)(2,1)S(1)} all-to-all(bf16[16,128,128]{2,1,0:T(8,128)(2,1)} %get-tuple-element.28), channel_id=1, replica_groups=mesh['dp'=32,'seq'=16] {'seq'}, dimensions={0} | all-to-all | bytes 1048576 | tf_op jit(solution)/shard_map/d_mixed_exchange/all_to_all | solution.py:454
  134.9 0.7 broadcast_in_dim.16
  135.6 7.0 %all-to-all-start.3 = ((f32[8,16,128]{2,1,0:T(8,128)}), f32[8,16,128]{2,1,0:T(8,128)S(1)}, u32[]{:S(2)}, u32[]{:S(2)}) async-start(f32[8,16,128]{2,1,0:T(8,128)} %broadcast_in_dim.16), calls=%async_computation.3 | async-start | bytes 131072 | tf_op jit(solution)/shard_map/small_sums/all_to_all | solution.py:462
  142.6 0.0 copy-done.2
  142.6 11.1 %backward.1 = bf16[32,112,128]{2,1,0:T(8,128)(2,1)} custom-call(bf16[16,128,128]{2,1,0:T(8,128)(2,1)} %copy-done.2, bf16[16,128,1536]{2,1,0:T(8,128)(2,1)} %bitcast.27, bf16[288,2304]{1,0:T(8,128)(2,1)} %get-tuple-element.29.qkvt_in, bf16[2304,96]{1,0:T(8,128)(2,1)} %get-tuple-element.30.v_in, bf16[16,384,128]{2,1,0:T(8,128)(2,1)} %get-tuple-element.31.soft_in), custom_call_target="tpu_custom_call" | custom-call | tf_op jit(solution)/shard_map/backward/pallas_call | solution.py:466
  153.7 0.0 all-to-all-done.3
  153.7 8.5 %all-to-all-start.4 = ((bf16[32,112,128]{2,1,0:T(8,128)(2,1)}), bf16[32,112,128]{2,1,0:T(8,128)(2,1)S(1)}, u32[]{:S(2)}, u32[]{:S(2)}) async-start(bf16[32,112,128]{2,1,0:T(8,128)(2,1)} %backward.1), calls=%async_computation.4 | async-start | bytes 1835008 | tf_op jit(solution)/shard_map/grad_exchange/all_to_all | solution.py:487
  162.2 10.2 %all-gather.1 = f32[64,128]{1,0:T(8,128)S(1)} all-gather(f32[16,128]{1,0:T(8,128)S(1)} %reduce_sum.28), channel_id=3, replica_groups={{0,128,256,384},{16,144,272,400},{32,160,288,416},{48,176,304,432},{64,..., dimensions={0}, use_global_device_ids=true | all-gather | bytes 40960 | tf_op jit(solution)/shard_map/small_gathers/all_gather | solution.py:490
  172.4 17.2 %all-gather.2 = f32[256,128]{1,0:T(8,128)S(1)} all-gather(f32[16,128]{1,0:T(8,128)S(1)} %reduce_sum.29), channel_id=4, replica_groups=mesh['dp'=32,'seq'=16] {'seq'}, dimensions={0}, use_global_device_ids=true | all-gather | bytes 139264 | tf_op jit(solution)/shard_map/small_gathers/all_gather | solution.py:491
  189.7 0.7 spread.1
  190.3 0.0 all-to-all-done.4.in_ref
  190.3 0.8 sum.1
  (8 shorter events, 0.1 us)
Async XLA Ops:
  7.2 2.2 %copy-start = (bf16[1,96,1536]{2,1,0:T(8,128)(2,1)S(1)}, bf16[1,96,1536]{2,1,0:T(8,128)(2,1)}, u32[]{:S(2)}) copy-start(bf16[1,96,1536]{2,1,0:T(8,128)(2,1)} %param.11) | copy-start | bytes 884740
  7.2 63.9 %all-gather.5.cloned.1.call-start = ((), (), s32[]{:S(2)}) async-start(), calls=%async_computation.5 | async-start | bytes 6684672 | tf_op jit(solution)/shard_map/gather/all_gather | solution.py:363
  7.2 1.0 copy-start.1
  37.5 7.8 %collective-permute-start = (bf16[8,96,384]{2,1,0:T(8,128)(2,1)S(1)}, bf16[8,96,384]{2,1,0:T(8,128)(2,1)S(1)}, u32[]{:S(2)}, u32[]{:S(2)}) collective-permute-start(bf16[8,96,384]{2,1,0:T(8,128)(2,1)S(1)} %all_to_all.25), channel_id=1, source_target_pairs={{0,1},{1,0},{2,3},{3,2},{4,5},{5,4},{6,7},{7,6},{8,9},{9,8},{10,11... | collective-permute-start | bytes 1769480 | tf_op jit(solution)/shard_map/w_out_columns/ppermute | solution.py:382
  45.4 37.6 %copy-start.4 = (bf16[16,96,384]{2,1,0:T(8,128)(2,1)}, bf16[16,96,384]{2,1,0:T(8,128)(2,1)S(1)}, u32[]{:S(2)}) copy-start(bf16[16,96,384]{2,1,0:T(8,128)(2,1)S(1)} %constant_dynamic-update-slice_fusion.own_ref) | copy-start | bytes 3538948
  45.4 17.6 %collective-permute-start.1 = (bf16[16,96,384]{2,1,0:T(8,128)(2,1)S(1)}, bf16[16,96,384]{2,1,0:T(8,128)(2,1)S(1)}, u32[]{:S(2)}, u32[]{:S(2)}) collective-permute-start(bf16[16,96,384]{2,1,0:T(8,128)(2,1)S(1)} %constant_dynamic-update-slice_fusion.own_ref), channel_id=1, source_target_pairs={{0,128},{1,385},{2,130},{3,387},{4,132},{5,389},{6,134},{7,391},{8... | collective-permute-start | bytes 3538952 | tf_op jit(solution)/shard_map/w_out_columns/ppermute | solution.py:388
  51.4 4.4 %collective-permute-start.2 = (bf16[16,1536]{1,0:T(8,128)(2,1)S(1)}, bf16[16,1536]{1,0:T(8,128)(2,1)S(1)}, u32[]{:S(2)}, u32[]{:S(2)}) collective-permute-start(bf16[16,1536]{1,0:T(8,128)(2,1)S(1)} %pad_maximum_fusion), channel_id=1, source_target_pairs={{0,1},{1,2},{2,3},{3,4},{4,5},{5,6},{6,7},{7,8},{8,9},{9,10},{10,1... | collective-permute-start | bytes 147464 | tf_op jit(solution)/shard_map/halo/ppermute | solution.py:369
  53.3 6.4 %collective-permute-start.3 = (bf16[16,1536]{1,0:T(8,128)(2,1)S(1)}, bf16[16,1536]{1,0:T(8,128)(2,1)S(1)}, u32[]{:S(2)}, u32[]{:S(2)}) collective-permute-start(bf16[16,1536]{1,0:T(8,128)(2,1)S(1)} %pad_maximum_fusion.1), channel_id=1, source_target_pairs={{1,0},{2,1},{3,2},{4,3},{5,4},{6,5},{7,6},{8,7},{9,8},{10,9},{11,1... | collective-permute-start | bytes 147464 | tf_op jit(solution)/shard_map/halo/ppermute | solution.py:370
  55.7 27.2 %copy-start.7 = (bf16[16,1536]{1,0:T(8,128)(2,1)}, bf16[16,1536]{1,0:T(8,128)(2,1)S(1)}, u32[]{:S(2)}) copy-start(bf16[16,1536]{1,0:T(8,128)(2,1)S(1)} %collective-permute-done.2.prev_in) | copy-start | bytes 147460
  59.7 23.2 %copy-start.8 = (bf16[16,1536]{1,0:T(8,128)(2,1)}, bf16[16,1536]{1,0:T(8,128)(2,1)S(1)}, u32[]{:S(2)}) copy-start(bf16[16,1536]{1,0:T(8,128)(2,1)S(1)} %collective-permute-done.3.next_in) | copy-start | bytes 147460
  63.0 20.0 %copy-start.3 = (bf16[16,96,384]{2,1,0:T(8,128)(2,1)}, bf16[16,96,384]{2,1,0:T(8,128)(2,1)S(1)}, u32[]{:S(2)}) copy-start(bf16[16,96,384]{2,1,0:T(8,128)(2,1)S(1)} %collective-permute-done.1.near_ref) | copy-start | bytes 3538948
  63.0 23.8 %collective-permute-start.5 = (bf16[8,96,384]{2,1,0:T(8,128)(2,1)S(1)}, bf16[8,96,384]{2,1,0:T(8,128)(2,1)}, u32[]{:S(2)}, u32[]{:S(2)}) collective-permute-start(bf16[8,96,384]{2,1,0:T(8,128)(2,1)S(1)} %slice.38), channel_id=1, source_target_pairs={{0,128},{1,385},{2,130},{3,387},{4,132},{5,389},{6,134},{7,391},{8... | collective-permute-start | bytes 1769480 | tf_op jit(solution)/shard_map/w_out_columns/ppermute | solution.py:391
  68.5 22.5 %collective-permute-start.4 = (bf16[16,96,384]{2,1,0:T(8,128)(2,1)S(1)}, bf16[16,96,384]{2,1,0:T(8,128)(2,1)}, u32[]{:S(2)}, u32[]{:S(2)}) collective-permute-start(bf16[16,96,384]{2,1,0:T(8,128)(2,1)S(1)} %collective-permute-done.1.near_ref), channel_id=1, source_target_pairs={{0,1},{1,0},{2,3},{3,2},{4,5},{5,4},{6,7},{7,6},{8,9},{9,8},{10,11... | collective-permute-start | bytes 3538952 | tf_op jit(solution)/shard_map/w_out_columns/ppermute | solution.py:390
  71.1 18.1 %copy-start.9 = (f32[1536]{0:T(1024)S(1)}, f32[1536]{0:T(1024)}, u32[]{:S(2)}) copy-start(f32[1536]{0:T(1024)} %param.13) | copy-start | bytes 18436
  71.1 18.7 %copy-start.10 = (f32[1536]{0:T(1024)S(1)}, f32[1536]{0:T(1024)}, u32[]{:S(2)}) copy-start(f32[1536]{0:T(1024)} %param.14) | copy-start | bytes 18436
  83.0 19.8 %all-to-all-start.1 = ((bf16[16,112,128]{2,1,0:T(8,128)(2,1)}), bf16[16,112,128]{2,1,0:T(8,128)(2,1)S(1)}, u32[]{:S(2)}, u32[]{:S(2)}) async-start(bf16[16,112,128]{2,1,0:T(8,128)(2,1)} %get-tuple-element.23), calls=%async_computation.1 | async-start | bytes 917504 | tf_op jit(solution)/shard_map/mixed_exchange/all_to_all | solution.py:421
  86.8 4.1 %collective-permute-start.6 = (bf16[8,96,384]{2,1,0:T(8,128)(2,1)}, bf16[8,96,384]{2,1,0:T(8,128)(2,1)S(1)}, u32[]{:S(2)}, u32[]{:S(2)}) collective-permute-start(bf16[8,96,384]{2,1,0:T(8,128)(2,1)} %collective-permute-done.5.far_ref), channel_id=1, source_target_pairs={{0,1},{1,0},{2,3},{3,2},{4,5},{5,4},{6,7},{7,6},{8,9},{9,8},{10,11... | collective-permute-start | bytes 1769480 | tf_op jit(solution)/shard_map/w_out_columns/ppermute | solution.py:392
  91.0 11.8 %copy-start.6 = (bf16[8,96,384]{2,1,0:T(8,128)(2,1)}, bf16[8,96,384]{2,1,0:T(8,128)(2,1)S(1)}, u32[]{:S(2)}) copy-start(bf16[8,96,384]{2,1,0:T(8,128)(2,1)S(1)} %collective-permute-done.6.twin_far_ref) | copy-start | bytes 1769476
  102.8 0.8 copy-start.5
  134.8 7.8 %copy-start.2 = (bf16[16,128,128]{2,1,0:T(8,128)(2,1)}, bf16[16,128,128]{2,1,0:T(8,128)(2,1)S(1)}, u32[]{:S(2)}) copy-start(bf16[16,128,128]{2,1,0:T(8,128)(2,1)S(1)} %all_to_all.26.in_ref) | copy-start | bytes 1572868
  135.6 18.1 %all-to-all-start.3 = ((f32[8,16,128]{2,1,0:T(8,128)}), f32[8,16,128]{2,1,0:T(8,128)S(1)}, u32[]{:S(2)}, u32[]{:S(2)}) async-start(f32[8,16,128]{2,1,0:T(8,128)} %broadcast_in_dim.16), calls=%async_computation.3 | async-start | bytes 131072 | tf_op jit(solution)/shard_map/small_sums/all_to_all | solution.py:462
  153.7 36.6 %all-to-all-start.4 = ((bf16[32,112,128]{2,1,0:T(8,128)(2,1)}), bf16[32,112,128]{2,1,0:T(8,128)(2,1)S(1)}, u32[]{:S(2)}, u32[]{:S(2)}) async-start(bf16[32,112,128]{2,1,0:T(8,128)(2,1)} %backward.1), calls=%async_computation.4 | async-start | bytes 1835008 | tf_op jit(solution)/shard_map/grad_exchange/all_to_all | solution.py:487
Sparse Core Ops, SparseCore 0:
  10.7 57.9 all-gather.4

commit v3 on v2

--- a/solution.py
+++ b/solution.py
@@ -29,11 +29,29 @@
     return lax.dot_general(a, b, ((dims[:1], dims[1:]), ((), ())), preferred_element_type=F32)
 
 
-def norm_kernel(x_ref, normed_ref):
-    values = x_ref[...].astype(F32)
-    center = values - jnp.mean(values, axis=-1, keepdims=True)
-    spread = jnp.mean(center * center, axis=-1, keepdims=True)
-    normed_ref[...] = (center * lax.rsqrt(spread + EPS)).astype(BF16)
+def norm_kernel(x_in, normed_out, x_ref, normed_ref, sems):
+    parts = sems.shape[1]
+    step = x_ref.shape[0] // parts
+    places = [pl.ds(c * step, step) for c in range(parts)]
+    takes = [
+        pltpu.make_async_copy(x_in.at[at], x_ref.at[at], sems.at[0, c])
+        for c, at in enumerate(places)
+    ]
+    gives = [
+        pltpu.make_async_copy(normed_ref.at[at], normed_out.at[at], sems.at[1, c])
+        for c, at in enumerate(places)
+    ]
+    for take in takes:
+        take.start()
+    for at, take, give in zip(places, takes, gives):
+        take.wait()
+        values = x_ref[at, :].astype(F32)
+        center = values - jnp.mean(values, axis=-1, keepdims=True)
+        spread = jnp.mean(center * center, axis=-1, keepdims=True)
+        normed_ref[at, :] = (center * lax.rsqrt(spread + EPS)).astype(BF16)
+        give.start()
+    for give in gives:
+        give.wait()
 
 
 def forward_kernel(
@@ -44,15 +62,12 @@
     hd = v_ref.shape[1]
     total = blocks * WIN
     per = blocks // sems.shape[0]
-    kept = [
-        pltpu.make_async_copy(qkvt_ref, qkvt_out, out_sems.at[0]),
-        pltpu.make_async_copy(v_ref, v_out, out_sems.at[1]),
-    ] + [
-        pltpu.make_async_copy(
-            soft_ref.at[pl.ds(c * per, per)], soft_out.at[pl.ds(c * per, per)], out_sems.at[2 + c]
-        )
-        for c in range(sems.shape[0])
-    ]
+    sends = []
+
+    def send(source, target):
+        sends.append(pltpu.make_async_copy(source, target, out_sems.at[len(sends)]))
+        sends[-1].start()
+
     copies = [
         pltpu.make_async_copy(
             gathered_ref.at[pl.ds(c * per, per)],
@@ -79,18 +94,6 @@
         v_ref[edge, :] = jnp.zeros((WIN, hd), BF16)
     mixed[0] = jnp.zeros(mixed.shape[1:], F32)
     mixed[blocks + 1] = jnp.zeros(mixed.shape[1:], F32)
-    wt = wt_ref[...]
-    for c, copy in enumerate(copies):
-        copy.wait()
-        rows = normed[c * per : (c + 1) * per].reshape(per * WIN, normed.shape[2])
-        part = dot(wt, rows, (1, 1))
-        at = slice(WIN + c * per * WIN, WIN + (c + 1) * per * WIN)
-        qkvt_ref[:, at] = part.astype(BF16)
-        k_ref[at, 0:hd] = part[hd : 2 * hd].T.astype(BF16)
-        v_ref[at, :] = part[2 * hd :].T.astype(BF16)
-
-    for copy in kept[:2]:
-        copy.start()
     column = lax.broadcasted_iota(jnp.int32, (1, WIN), 1)
     scale = hd ** (-0.5)
 
@@ -111,9 +114,24 @@
         out_ref[i, 0:hd, :] = result.astype(BF16)
         return carry
 
-    for c in range(sems.shape[0]):
-        lax.fori_loop(c * per, (c + 1) * per, attend, 0, unroll=True)
-        kept[2 + c].start()
+    wt = wt_ref[...]
+    for c, copy in enumerate(copies):
+        copy.wait()
+        rows = normed[c * per : (c + 1) * per].reshape(per * WIN, normed.shape[2])
+        part = dot(wt, rows, (1, 1))
+        at = slice(WIN + c * per * WIN, WIN + (c + 1) * per * WIN)
+        qkvt_ref[:, at] = part.astype(BF16)
+        k_ref[at, 0:hd] = part[hd : 2 * hd].T.astype(BF16)
+        v_ref[at, :] = part[2 * hd :].T.astype(BF16)
+        final = c == len(copies) - 1
+        low, high = at.start - WIN * (c == 0), at.stop + WIN * final
+        done = pl.ds(low, high - low)
+        send(qkvt_ref.at[:, done], qkvt_out.at[:, done])
+        send(v_ref.at[done], v_out.at[done])
+        first, stop = max(c * per - 1, 0), (c + 1) * per - 1 + final
+        lax.fori_loop(first, stop, attend, 0, unroll=True)
+        done = pl.ds(first, stop - first)
+        send(soft_ref.at[done], soft_out.at[done])
 
     def edges(i, carry):
         both = jnp.where(column < EDGE, mixed[i + 2], mixed[i]).T
@@ -122,13 +140,13 @@
         return carry
 
     lax.fori_loop(0, blocks, edges, 0, unroll=4)
-    for copy in kept:
+    for copy in sends:
         copy.wait()
 
 
 def middle_kernel(
     total, place_ref, mix_in, x_in, g_in, prev_in, next_in, own_ref, near_ref, twin_ref, far_ref,
-    twin_far_ref, taps_ref, scale_ref, shift_ref, layer_out, out_ref, mix_ref, x_ref, g_ref,
+    taps_ref, scale_ref, shift_ref, layer_out, out_ref, mix_ref, x_ref, g_ref,
     prev_ref, next_ref, layer_ref, weight, d_hidden, masked, d_conv, small, sems, more_sems
 ):
     inputs = [
@@ -150,7 +168,7 @@
         (0, own_ref.at[first], own_ref.at[last]),
         (2 * core - 1, near_ref.at[first], near_ref.at[last]),
         (1 - 2 * core, twin_ref.at[last], twin_ref.at[first]),
-        (2, far_ref, twin_far_ref),
+        (2, far_ref.at[first], far_ref.at[last]),
     )
 
     def fetch(quarter, lower, upper):
@@ -232,40 +250,48 @@
         d_mixed = jnp.where(column < length, d_mixed, 0.0).astype(BF16)
         for j in range(group):
             out_ref[order[h + j], 0:hd, :] = d_mixed[j * hd : (j + 1) * hd]
-    high = small[...].astype(BF16)
-    low = (small[...] - high.astype(F32)).astype(BF16)
-    more = small.shape[0]
+    sums = small[...].astype(BF16)
     for h in range(heads):
         if (h + 1) * LANES <= width:
-            at = slice(h * LANES, (h + 1) * LANES)
-            out_ref[h, hd : hd + more, :] = high[:, at]
-            out_ref[h, hd + more :, :] = low[:, at]
+            out_ref[h, hd:, :] = sums[:, h * LANES : (h + 1) * LANES]
         else:
-            out_ref[h, hd:, :] = jnp.zeros((2 * more, rows), BF16)
+            out_ref[h, hd:, :] = jnp.zeros((small.shape[0], rows), BF16)
     result.wait()
 
 
 def backward_kernel(
-    shares, in_ref, gathered_ref, qkvt_in, v_in, soft_in, out_ref,
-    normed, d_query, d_key, d_value, joined, grad, qkvt_ref, v_ref, soft_ref, sems
+    shares, d_mixed_in, gathered_ref, qkvt_in, v_in, soft_in, message_out,
+    normed, d_query, d_key, d_value, joined, grad, qkvt_ref, v_ref, soft_ref, in_ref, out_ref,
+    sems, fetch_sems, out_sems
 ):
     blocks, width = gathered_ref.shape[0], gathered_ref.shape[2]
     hd = v_ref.shape[1]
     total = blocks * WIN
-    groups = sems.shape[0] - 3
+    groups = sems.shape[0]
     per = blocks // groups
-    copies = [
-        pltpu.make_async_copy(v_in, v_ref, sems.at[0]),
-        pltpu.make_async_copy(qkvt_in, qkvt_ref, sems.at[1]),
-    ] + [
+    copies = []
+    for c in range(groups):
+        low, high = (2 + c * per) * WIN * (c > 0), (2 + (c + 1) * per) * WIN
+        window, own = pl.ds(low, high - low), pl.ds(c * per, per)
+        copies.append([
+            pltpu.make_async_copy(v_in.at[window], v_ref.at[window], sems.at[c, 0]),
+            pltpu.make_async_copy(d_mixed_in.at[own], in_ref.at[own], sems.at[c, 1]),
+            pltpu.make_async_copy(soft_in.at[own], soft_ref.at[own], sems.at[c, 2]),
+            pltpu.make_async_copy(qkvt_in.at[:, window], qkvt_ref.at[:, window], sems.at[c, 3]),
+        ])
+    for group in copies:
+        for copy in group:
+            copy.start()
+    steps = fetch_sems.shape[0]
+    step = width // steps
+    fetches = [
         pltpu.make_async_copy(
-            soft_in.at[pl.ds(c * per, per)], soft_ref.at[pl.ds(c * per, per)], sems.at[2 + c]
-        )
-        for c in range(groups)
+            gathered_ref.at[:, :, pl.ds(c * step, step)],
+            normed.at[:, :, pl.ds(c * step, step)],
+            fetch_sems.at[c],
+        )
+        for c in range(steps)
     ]
-    for copy in copies:
-        copy.start()
-    fetch = pltpu.make_async_copy(gathered_ref, normed, sems.at[2 + groups])
     d_key[...] = jnp.zeros(d_key.shape, F32)
     d_value[...] = jnp.zeros(d_value.shape, F32)
     scale = hd ** (-0.5)
@@ -285,37 +311,44 @@
         d_value[:, window] += dot(d_mixed, soft, (1, 1))
         return carry
 
-    copies[0].wait()
-    copies[1].wait()
-    fetch.start()
-    for c in range(groups):
-        copies[2 + c].wait()
+    for c, group in enumerate(copies):
+        for copy in group:
+            copy.wait()
+        if c == 0:
+            for fetch in fetches:
+                fetch.start()
         lax.fori_loop(c * per, (c + 1) * per, attend, 0, unroll=True)
     joined[0:hd, :] = d_query[...]
     joined[hd : 2 * hd, :] = d_key[:, WIN : WIN + total].astype(BF16)
     joined[2 * hd :, :] = d_value[:, WIN : WIN + total].astype(BF16)
-    fetch.wait()
     rest = 3 * hd - 2 * LANES
     repeats = LANES // rest
-    step = 512
-    for c in range(width // step):
-        at = slice(c * step, (c + 1) * step)
-        rows = normed[:, :, at].reshape(total, step)
-        part = dot(joined[...], rows, (1, 0))
-        tail = part[2 * LANES :]
-        grad[at, :] = jnp.concatenate([part[: 2 * LANES]] + [tail] * repeats, axis=0).T
     share = width // shares
     third = share // (repeats - 1)
     lane = lax.broadcasted_iota(jnp.int32, (1, LANES), 1) // rest
-    for d in range(shares):
-        at = slice(d * share, (d + 1) * share)
-        out_ref[d, 0:share, :] = grad[at, 0:LANES].astype(BF16)
-        out_ref[d, share : 2 * share, :] = grad[at, LANES : 2 * LANES].astype(BF16)
-        packed = jnp.zeros((third, LANES), F32)
-        for j in range(repeats - 1):
-            first = d * share + j * third
-            packed = jnp.where(lane == j, grad[first : first + third, 2 * LANES :], packed)
-        out_ref[d, 2 * share :, :] = packed.astype(BF16)
+    each = step // share
+    sends = []
+    for c, fetch in enumerate(fetches):
+        fetch.wait()
+        rows = normed[:, :, c * step : (c + 1) * step].reshape(total, step)
+        part = dot(joined[...], rows, (1, 0))
+        tail = part[2 * LANES :]
+        grad[c] = jnp.concatenate([part[: 2 * LANES]] + [tail] * repeats, axis=0).T
+        for j in range(each):
+            d = c * each + j
+            at = slice(j * share, (j + 1) * share)
+            out_ref[d, 0:share, :] = grad[c, at, 0:LANES].astype(BF16)
+            out_ref[d, share : 2 * share, :] = grad[c, at, LANES : 2 * LANES].astype(BF16)
+            packed = jnp.zeros((third, LANES), F32)
+            for i in range(repeats - 1):
+                first = j * share + i * third
+                packed = jnp.where(lane == i, grad[c, first : first + third, 2 * LANES :], packed)
+            out_ref[d, 2 * share :, :] = packed.astype(BF16)
+        done = pl.ds(c * each, each)
+        sends.append(pltpu.make_async_copy(out_ref.at[done], message_out.at[done], out_sems.at[c]))
+        sends[-1].start()
+    for send in sends:
+        send.wait()
 
 
 def sum_kernel(in_ref, grad_ref):
@@ -354,10 +387,15 @@
     with jax.named_scope("norm"):
         normed = pl.pallas_call(
             norm_kernel,
-            in_specs=[VMEM],
-            out_specs=VMEM,
+            in_specs=[HBM],
+            out_specs=HBM,
             out_shape=shape((rows, width), BF16),
-            compiler_params=params(16),
+            scratch_shapes=[
+                pltpu.VMEM((rows, width), BF16),
+                pltpu.VMEM((rows, width), BF16),
+                pltpu.SemaphoreType.DMA((2, 2)),
+            ],
+            compiler_params=params(60),
         )(x)
     with jax.named_scope("gather"):
         gathered = lax.all_gather(normed, "seq")
@@ -386,10 +424,13 @@
 
         ring = [(d * blocks + i, onward(d, i)) for d in range(shares) for i in range(blocks)]
         near = lax.ppermute(columns, ("dp", "seq"), ring)
-        near, before, after = lax.optimization_barrier((near, before, after))
+        place = jnp.stack([lax.axis_index("seq"), lengths[0], lax.axis_index("dp") // per])
+        gain, offset = bn_scale.reshape(1, width), bn_shift.reshape(1, width)
+        near, before, after, place, gain, offset = lax.optimization_barrier(
+            (near, before, after, place, gain, offset)
+        )
         twin = lax.ppermute(near, "seq", twins)
-        far = lax.ppermute(near[: blocks // 2], ("dp", "seq"), ring)
-        twin_far = lax.ppermute(far, "seq", twins)
+        far = lax.ppermute(near, ("dp", "seq"), ring)
     gathered, near = lax.optimization_barrier((gathered, near))
     wt = w_qkv.reshape(width, 3 * hd).T
 
@@ -413,22 +454,22 @@
                 pltpu.VMEM((blocks, 3 * WIN, WIN), BF16),
                 pltpu.VMEM((3 * WIN, WIN), F32),
                 pltpu.SemaphoreType.DMA((4,)),
-                pltpu.SemaphoreType.DMA((6,)),
+                pltpu.SemaphoreType.DMA((12,)),
             ],
-            compiler_params=params(58),
+            compiler_params=params(54),
         )(lengths, gathered, wt)
+    mixed, twin, far = lax.optimization_barrier((mixed, twin, far))
     with jax.named_scope("mixed_exchange"):
         mixed = lax.all_to_all(mixed, "seq", 0, 0)
 
     with jax.named_scope("middle"):
-        place = jnp.stack([lax.axis_index("seq"), lengths[0], lax.axis_index("dp") // per])
         layer_out, d_mixed = pl.pallas_call(
             functools.partial(middle_kernel, total),
-            in_specs=[SMEM] + [HBM] * 10 + [VMEM] * 3,
+            in_specs=[SMEM] + [HBM] * 9 + [VMEM] * 3,
             out_specs=[HBM, VMEM],
             out_shape=[
                 shape((rows, width), BF16),
-                shape((blocks, hd + 2 * small_rows, rows), BF16),
+                shape((blocks, hd + small_rows, rows), BF16),
             ],
             scratch_shapes=[
                 pltpu.VMEM(mixed.shape, BF16),
@@ -445,10 +486,9 @@
                 pltpu.SemaphoreType.DMA((firsts, 2)),
                 pltpu.SemaphoreType.DMA((6,)),
             ],
-            compiler_params=params(60),
+            compiler_params=params(30),
         )(
-            place, mixed, x, g, before, after, columns, near, twin, far, twin_far, kernel,
-            bn_scale.reshape(1, width), bn_shift.reshape(1, width),
+            place, mixed, x, g, before, after, columns, near, twin, far, kernel, gain, offset,
         )
     with jax.named_scope("d_mixed_exchange"):
         d_mixed = lax.all_to_all(d_mixed, "seq", 0, 0)
@@ -458,15 +498,15 @@
     across = [[i * per + j for i in range(firsts)] for j in range(per)]
     along = [[i * per + j for j in range(per)] for i in range(firsts)]
     with jax.named_scope("small_sums"):
-        small = jnp.sum(d_mixed[:, hd:].astype(F32).reshape(2 * blocks, small_rows, LANES), axis=0)
+        small = jnp.sum(d_mixed[:, hd:].astype(F32), axis=0)
         small = lax.all_to_all(
             jnp.broadcast_to(small, (per,) + small.shape), "dp", 0, 0, axis_index_groups=along
         )
     with jax.named_scope("backward"):
         messages = pl.pallas_call(
             functools.partial(backward_kernel, shares),
-            in_specs=[VMEM] + [HBM] * 4,
-            out_specs=VMEM,
+            in_specs=[HBM] * 5,
+            out_specs=HBM,
             out_shape=shape((shares, 2 * share + third, LANES), BF16),
             scratch_shapes=[
                 pltpu.VMEM((blocks, WIN, width), BF16),
@@ -474,11 +514,15 @@
                 pltpu.VMEM((hd, total + 2 * WIN), F32),
                 pltpu.VMEM((hd, total + 2 * WIN), F32),
                 pltpu.VMEM((3 * hd, total), BF16),
-                pltpu.VMEM((width, 3 * LANES), F32),
+                pltpu.VMEM((4, width // 4, 3 * LANES), F32),
                 pltpu.VMEM((3 * hd, total + 2 * WIN), BF16),
                 pltpu.VMEM((total + 2 * WIN, hd), BF16),
                 pltpu.VMEM((blocks, 3 * WIN, WIN), BF16),
-                pltpu.SemaphoreType.DMA((7,)),
+                pltpu.VMEM((blocks, hd + small_rows, WIN), BF16),
+                pltpu.VMEM((shares, 2 * share + third, LANES), BF16),
+                pltpu.SemaphoreType.DMA((4, 4)),
+                pltpu.SemaphoreType.DMA((4,)),
+                pltpu.SemaphoreType.DMA((4,)),
             ],
             compiler_params=params(56),
         )(d_mixed, gathered, qkvt, v, soft)

time: 199 us -> 194 us (0.975)
  blocking collectives: 75.6 us -> 95.6 us
  waiting for transfers between devices: 20.8 us -> 7.05 us
  starting transfers between devices: 43.8 us -> 37 us
  local copies, waits for them, and re-layouts: 5.61 us -> 1.69 us
    all_to_all x0 -> x1, blocking collectives: none -> 21.8 us  [on_device(): mixed = lax.all_to_all(mixed, 'seq', 0, 0)]
    all_to_all x1 -> x0, waiting for transfers between devices: 11.8 us -> none  [on_device(): mixed = lax.all_to_all(mixed, 'seq', 0, 0)]
    all_to_all x1 -> x0, starting transfers between devices: 3.86 us -> none  [on_device(): mixed = lax.all_to_all(mixed, 'seq', 0, 0)]
    ppermute x2 -> x1, starting transfers between devices: 7.74 us -> 5.41 us  [on_device(): far = lax.ppermute(near, ('dp', 'seq'), ring)]
    pallas_call x1, Pallas kernels: 11.1 us -> 9.04 us  [on_device(): pl.pallas_call(functools.partial(middle_kernel, total), in_specs=[SMEM] +...]
  transfers between devices with their start and end apart: 11 -> 9, of which waited for: 4 -> 3; matrix products, arithmetic and copies ran while one was open for 2% -> 1% of each run, Pallas kernels for 12% -> 12%
where the time goes in v3:
time: 194 us
  blocking collectives  95.6 us (49%)
  starting transfers between devices  37 us (19%)
  Pallas kernels  35.4 us (18%)
  between operations  14.9 us (8%)
  waiting for transfers between devices  7.05 us (4%)
  other arithmetic  1.96 us (1%)
    all_to_all x1, blocking collectives, on_device(): columns = lax.all_to_all(columns, 'seq', 0, 0, axis_index_groups=same)  27.9 us
    all_to_all x1, blocking collectives, on_device(): mixed = lax.all_to_all(mixed, 'seq', 0, 0)  21.8 us
    all_to_all x1, blocking collectives, on_device(): d_mixed = lax.all_to_all(d_mixed, 'seq', 0, 0)  18.6 us
    all_gather x1, blocking collectives, on_device(): small = lax.all_gather(small, 'seq')  17.1 us
    pallas_call x1, Pallas kernels, on_device(): pl.pallas_call(forward_kernel, in_specs=[SMEM, HBM, VMEM], out_specs=[VME...  11.7 us
    pallas_call x1, Pallas kernels, on_device(): pl.pallas_call(functools.partial(backward_kernel, shares), in_specs=[HBM]...  11.1 us
    all_gather x1, blocking collectives, on_device(): lax.all_gather(small, 'dp', axis_index_groups=across)  10.2 us
    pallas_call x1, Pallas kernels, on_device(): pl.pallas_call(functools.partial(middle_kernel, total), in_specs=[SMEM] +...  9.04 us
  transfers between devices with their start and end apart: 9, of which 3 were waited for; matrix products, arithmetic and copies ran while one was open for 1% of the time, Pallas kernels for 12%

profile of v3, /device:TPU:1, one launch (start us, length us, event | category | flops | bytes accessed | tf_op | source)
XLA Modules:
  0.0 193.7 jit_solution(15692222623502518812)
XLA Ops:
  7.2 0.0 copy-start
  7.2 0.0 all-gather.5.cloned.1.call-start
  7.2 2.1 %norm.1 = bf16[128,1536]{1,0:T(8,128)(2,1)} custom-call(bf16[128,1536]{1,0:T(8,128)(2,1)} %bitcast.21), custom_call_target="tpu_custom_call" | custom-call | tf_op jit(solution)/shard_map/norm/pallas_call | solution.py:388
  9.4 0.0 all-gather.5.cloned.1.call-update
  9.4 0.0 copy-done
  9.4 0.1 broadcast_in_dim.14
  9.5 27.9 %all_to_all.25 = bf16[8,96,384]{2,1,0:T(8,128)(2,1)S(1)} all-to-all(bf16[8,96,384]{2,1,0:T(8,128)(2,1)S(1)} %broadcast_in_dim.14), channel_id=1, replica_groups={{0,2,4,6,8,10,12,14},{1,3,5,7,9,11,13,15},{16,18,20,22,24,26,28,30},{17..., dimensions={0} | all-to-all | bytes 1179648 | tf_op jit(solution)/shard_map/w_out_columns/all_to_all | solution.py:419
  37.4 0.0 copy-start.1
  37.4 0.0 copy-start.2
  37.4 0.0 copy-start.6
  37.4 6.4 %collective-permute-start = (bf16[8,96,384]{2,1,0:T(8,128)(2,1)S(1)}, bf16[8,96,384]{2,1,0:T(8,128)(2,1)S(1)}, u32[]{:S(2)}, u32[]{:S(2)}) collective-permute-start(bf16[8,96,384]{2,1,0:T(8,128)(2,1)S(1)} %all_to_all.25), channel_id=1, source_target_pairs={{0,1},{1,0},{2,3},{3,2},{4,5},{5,4},{6,7},{7,6},{8,9},{9,8},{10,11... | collective-permute-start | bytes 1769480 | tf_op jit(solution)/shard_map/w_out_columns/ppermute | solution.py:420
  43.8 0.1 constant_dynamic-update-slice_fusion.1
  43.9 1.5 collective-permute-done
  45.4 0.1 constant_dynamic-update-slice_fusion.own_ref
  45.5 4.4 %collective-permute-start.1 = (bf16[16,96,384]{2,1,0:T(8,128)(2,1)S(1)}, bf16[16,96,384]{2,1,0:T(8,128)(2,1)S(1)}, u32[]{:S(2)}, u32[]{:S(2)}) collective-permute-start(bf16[16,96,384]{2,1,0:T(8,128)(2,1)S(1)} %constant_dynamic-update-slice_fusion.own_ref), channel_id=1, source_target_pairs={{0,128},{1,385},{2,130},{3,387},{4,132},{5,389},{6,134},{7,391},{8... | collective-permute-start | bytes 3538952 | tf_op jit(solution)/shard_map/w_out_columns/ppermute | solution.py:426
  49.9 0.0 copy-done.1
  49.9 0.0 copy-done.2
  50.0 0.6 pad_maximum_fusion
  50.6 1.9 collective-permute-start.2
  52.5 0.6 pad_maximum_fusion.1
  53.1 2.4 %collective-permute-start.3 = (bf16[16,1536]{1,0:T(8,128)(2,1)}, bf16[16,1536]{1,0:T(8,128)(2,1)S(1)}, u32[]{:S(2)}, u32[]{:S(2)}) collective-permute-start(bf16[16,1536]{1,0:T(8,128)(2,1)} %pad_maximum_fusion.1), channel_id=1, source_target_pairs={{1,0},{2,1},{3,2},{4,3},{5,4},{6,5},{7,6},{8,7},{9,8},{10,9},{11,1... | collective-permute-start | bytes 147464 | tf_op jit(solution)/shard_map/halo/ppermute | solution.py:408
  56.2 0.7 pad_add_fusion.place_ref
  56.9 0.0 copy-done.6
  56.9 0.7 reshape.24.shift_ref
  57.6 0.0 collective-permute-done.2.prev_in
  57.6 2.4 %collective-permute-done.3.next_in = bf16[16,1536]{1,0:T(8,128)(2,1)S(1)} collective-permute-done((bf16[16,1536]{1,0:T(8,128)(2,1)}, bf16[16,1536]{1,0:T(8,128)(2,1)S(1)}, u32[]{:S(2)}, u32[]{:S(2)}) %collective-permute-start.3) | collective-permute-done | bytes 49184 | tf_op jit(solution)/shard_map/halo/ppermute | solution.py:408
  59.9 3.1 %collective-permute-done.1.near_ref = bf16[16,96,384]{2,1,0:T(8,128)(2,1)S(1)} collective-permute-done((bf16[16,96,384]{2,1,0:T(8,128)(2,1)S(1)}, bf16[16,96,384]{2,1,0:T(8,128)(2,1)S(1)}, u32[]{:S(2)}, u32[]{:S(2)}) %collective-permute-start.1) | collective-permute-done | bytes 1179680 | tf_op jit(solution)/shard_map/w_out_columns/ppermute | solution.py:426
  63.0 5.4 %collective-permute-start.5 = (bf16[16,96,384]{2,1,0:T(8,128)(2,1)S(1)}, bf16[16,96,384]{2,1,0:T(8,128)(2,1)}, u32[]{:S(2)}, u32[]{:S(2)}) collective-permute-start(bf16[16,96,384]{2,1,0:T(8,128)(2,1)S(1)} %collective-permute-done.1.near_ref), channel_id=1, source_target_pairs={{0,128},{1,385},{2,130},{3,387},{4,132},{5,389},{6,134},{7,391},{8... | collective-permute-start | bytes 3538952 | tf_op jit(solution)/shard_map/w_out_columns/ppermute | solution.py:433
  68.5 1.9 collective-permute-start.4
  70.4 0.0 all-gather.5.cloned.1.call-done
  70.4 0.0 copy-start.3
  70.4 0.0 copy-start.4
  70.4 11.7 %forward.1 = (bf16[16,112,128]{2,1,0:T(8,128)(2,1)}, bf16[288,2304]{1,0:T(8,128)(2,1)}, bf16[2304,96]{1,0:T(8,128)(2,1)}, bf16[16,384,128]{2,1,0:T(8,128)(2,1)}) custom-call(s32[1]{0:T(128)S(6)} %copy.14.len_ref, bf16[16,128,1536]{2,1,0:T(8,128)(2,1)} %bitcast.25, bf16[288,1536]{1,0:T(8,128)(2,1)} %bitcast.27), custom_call_target="tpu_custom_call" | custom-call | tf_op jit(solution)/shard_map/forward/pallas_call | solution.py:438
  82.1 0.0 collective-permute-done.5.far_ref
  82.1 0.0 collective-permute-done.4.twin_ref
  82.2 21.8 %all_to_all.26.mix_in = bf16[16,112,128]{2,1,0:T(8,128)(2,1)S(1)} all-to-all(bf16[16,112,128]{2,1,0:T(8,128)(2,1)} %get-tuple-element.31), channel_id=1, replica_groups=mesh['dp'=32,'seq'=16] {'seq'}, dimensions={0} | all-to-all | bytes 917504 | tf_op jit(solution)/shard_map/mixed_exchange/all_to_all | solution.py:463
  103.9 0.0 copy-done.3
  103.9 0.0 copy-done.4
  103.9 9.0 %middle.1 = (bf16[128,1536]{1,0:T(8,128)(2,1)}, bf16[16,112,128]{2,1,0:T(8,128)(2,1)S(1)}) custom-call(s32[3]{0:T(128)S(1)} %copy-done.4, bf16[16,112,128]{2,1,0:T(8,128)(2,1)S(1)} %all_to_all.26.mix_in, bf16[128,1536]{1,0:T(8,128)(2,1)S(1)} %bitcast.22, bf16[128,1536]{1,0:T(8,128)(2,1)S(1)} %bitcast.24, ...), custom_call_target="tpu_custom_call" | custom-call | tf_op jit(solution)/shard_map/middle/pallas_call | solution.py:466
  113.0 18.6 %all_to_all.27.d_mixed_in = bf16[16,112,128]{2,1,0:T(8,128)(2,1)S(1)} all-to-all(bf16[16,112,128]{2,1,0:T(8,128)(2,1)S(1)} %get-tuple-element.40), channel_id=1, replica_groups=mesh['dp'=32,'seq'=16] {'seq'}, dimensions={0} | all-to-all | bytes 917504 | tf_op jit(solution)/shard_map/d_mixed_exchange/all_to_all | solution.py:494
  131.6 0.0 copy-start.5
  131.6 0.7 broadcast_in_dim.16
  132.3 7.1 %all-to-all-start.3 = ((f32[8,16,128]{2,1,0:T(8,128)}), f32[8,16,128]{2,1,0:T(8,128)S(1)}, u32[]{:S(2)}, u32[]{:S(2)}) async-start(f32[8,16,128]{2,1,0:T(8,128)} %broadcast_in_dim.16), calls=%async_computation.3 | async-start | bytes 131072 | tf_op jit(solution)/shard_map/small_sums/all_to_all | solution.py:502
  139.4 0.0 copy-done.5
  139.4 11.1 %backward.1 = bf16[32,112,128]{2,1,0:T(8,128)(2,1)} custom-call(bf16[16,112,128]{2,1,0:T(8,128)(2,1)} %copy-done.5, bf16[16,128,1536]{2,1,0:T(8,128)(2,1)} %bitcast.26, bf16[288,2304]{1,0:T(8,128)(2,1)} %get-tuple-element.41.qkvt_in, bf16[2304,96]{1,0:T(8,128)(2,1)} %get-tuple-element.42.v_in, bf16[16,384,128]{2,1,0:T(8,128)(2,1)} %get-tuple-element.43.soft_in), custom_call_target="tpu_custom_call" | custom-call | tf_op jit(solution)/shard_map/backward/pallas_call | solution.py:506
  150.5 0.0 all-to-all-done.3
  150.5 7.5 %all-to-all-start.4 = ((bf16[32,112,128]{2,1,0:T(8,128)(2,1)}), bf16[32,112,128]{2,1,0:T(8,128)(2,1)S(1)}, u32[]{:S(2)}, u32[]{:S(2)}) async-start(bf16[32,112,128]{2,1,0:T(8,128)(2,1)} %backward.1), calls=%async_computation.4 | async-start | bytes 1835008 | tf_op jit(solution)/shard_map/grad_exchange/all_to_all | solution.py:531
  158.1 10.2 %all-gather.1 = f32[64,128]{1,0:T(8,128)S(1)} all-gather(f32[16,128]{1,0:T(8,128)S(1)} %reduce_sum.28), channel_id=3, replica_groups={{0,128,256,384},{16,144,272,400},{32,160,288,416},{48,176,304,432},{64,..., dimensions={0}, use_global_device_ids=true | all-gather | bytes 40960 | tf_op jit(solution)/shard_map/small_gathers/all_gather | solution.py:534
  168.2 17.1 %all-gather.2 = f32[256,128]{1,0:T(8,128)S(1)} all-gather(f32[16,128]{1,0:T(8,128)S(1)} %reduce_sum.29), channel_id=4, replica_groups=mesh['dp'=32,'seq'=16] {'seq'}, dimensions={0}, use_global_device_ids=true | all-gather | bytes 139264 | tf_op jit(solution)/shard_map/small_gathers/all_gather | solution.py:535
  185.3 0.7 spread.1
  186.0 0.0 all-to-all-done.4.in_ref
  186.0 0.8 sum.1
  (7 shorter events, 0.1 us)
Async XLA Ops:
  7.2 2.2 %copy-start = (bf16[1,96,1536]{2,1,0:T(8,128)(2,1)S(1)}, bf16[1,96,1536]{2,1,0:T(8,128)(2,1)}, u32[]{:S(2)}) copy-start(bf16[1,96,1536]{2,1,0:T(8,128)(2,1)} %param.11) | copy-start | bytes 884740
  7.2 63.2 %all-gather.5.cloned.1.call-start = ((), (), s32[]{:S(2)}) async-start(), calls=%async_computation.5 | async-start | bytes 6684672 | tf_op jit(solution)/shard_map/gather/all_gather | solution.py:401
  37.4 12.5 %copy-start.1 = (bf16[1,128,1536]{2,1,0:T(8,128)(2,1)S(1)}, bf16[1,128,1536]{2,1,0:T(8,128)(2,1)}, u32[]{:S(2)}) copy-start(bf16[1,128,1536]{2,1,0:T(8,128)(2,1)} %param.8) | copy-start | bytes 1179652
  37.4 12.5 %copy-start.2 = (bf16[1,128,1536]{2,1,0:T(8,128)(2,1)S(1)}, bf16[1,128,1536]{2,1,0:T(8,128)(2,1)}, u32[]{:S(2)}) copy-start(bf16[1,128,1536]{2,1,0:T(8,128)(2,1)} %param.15) | copy-start | bytes 1179652
  37.4 19.4 %copy-start.6 = (f32[1536]{0:T(1024)S(1)}, f32[1536]{0:T(1024)}, u32[]{:S(2)}) copy-start(f32[1536]{0:T(1024)} %param.13) | copy-start | bytes 18436
  37.4 8.0 %collective-permute-start = (bf16[8,96,384]{2,1,0:T(8,128)(2,1)S(1)}, bf16[8,96,384]{2,1,0:T(8,128)(2,1)S(1)}, u32[]{:S(2)}, u32[]{:S(2)}) collective-permute-start(bf16[8,96,384]{2,1,0:T(8,128)(2,1)S(1)} %all_to_all.25), channel_id=1, source_target_pairs={{0,1},{1,0},{2,3},{3,2},{4,5},{5,4},{6,7},{7,6},{8,9},{9,8},{10,11... | collective-permute-start | bytes 1769480 | tf_op jit(solution)/shard_map/w_out_columns/ppermute | solution.py:420
  45.5 17.5 %collective-permute-start.1 = (bf16[16,96,384]{2,1,0:T(8,128)(2,1)S(1)}, bf16[16,96,384]{2,1,0:T(8,128)(2,1)S(1)}, u32[]{:S(2)}, u32[]{:S(2)}) collective-permute-start(bf16[16,96,384]{2,1,0:T(8,128)(2,1)S(1)} %constant_dynamic-update-slice_fusion.own_ref), channel_id=1, source_target_pairs={{0,128},{1,385},{2,130},{3,387},{4,132},{5,389},{6,134},{7,391},{8... | collective-permute-start | bytes 3538952 | tf_op jit(solution)/shard_map/w_out_columns/ppermute | solution.py:426
  50.6 7.0 %collective-permute-start.2 = (bf16[16,1536]{1,0:T(8,128)(2,1)}, bf16[16,1536]{1,0:T(8,128)(2,1)S(1)}, u32[]{:S(2)}, u32[]{:S(2)}) collective-permute-start(bf16[16,1536]{1,0:T(8,128)(2,1)} %pad_maximum_fusion), channel_id=1, source_target_pairs={{0,1},{1,2},{2,3},{3,4},{4,5},{5,6},{6,7},{7,8},{8,9},{9,10},{10,1... | collective-permute-start | bytes 147464 | tf_op jit(solution)/shard_map/halo/ppermute | solution.py:407
  53.1 6.8 %collective-permute-start.3 = (bf16[16,1536]{1,0:T(8,128)(2,1)}, bf16[16,1536]{1,0:T(8,128)(2,1)S(1)}, u32[]{:S(2)}, u32[]{:S(2)}) collective-permute-start(bf16[16,1536]{1,0:T(8,128)(2,1)} %pad_maximum_fusion.1), channel_id=1, source_target_pairs={{1,0},{2,1},{3,2},{4,3},{5,4},{6,5},{7,6},{8,7},{9,8},{10,9},{11,1... | collective-permute-start | bytes 147464 | tf_op jit(solution)/shard_map/halo/ppermute | solution.py:408
  63.0 19.1 %collective-permute-start.5 = (bf16[16,96,384]{2,1,0:T(8,128)(2,1)S(1)}, bf16[16,96,384]{2,1,0:T(8,128)(2,1)}, u32[]{:S(2)}, u32[]{:S(2)}) collective-permute-start(bf16[16,96,384]{2,1,0:T(8,128)(2,1)S(1)} %collective-permute-done.1.near_ref), channel_id=1, source_target_pairs={{0,128},{1,385},{2,130},{3,387},{4,132},{5,389},{6,134},{7,391},{8... | collective-permute-start | bytes 3538952 | tf_op jit(solution)/shard_map/w_out_columns/ppermute | solution.py:433
  68.5 13.7 %collective-permute-start.4 = (bf16[16,96,384]{2,1,0:T(8,128)(2,1)S(1)}, bf16[16,96,384]{2,1,0:T(8,128)(2,1)}, u32[]{:S(2)}, u32[]{:S(2)}) collective-permute-start(bf16[16,96,384]{2,1,0:T(8,128)(2,1)S(1)} %collective-permute-done.1.near_ref), channel_id=1, source_target_pairs={{0,1},{1,0},{2,3},{3,2},{4,5},{5,4},{6,7},{7,6},{8,9},{9,8},{10,11... | collective-permute-start | bytes 3538952 | tf_op jit(solution)/shard_map/w_out_columns/ppermute | solution.py:432
  70.4 33.5 %copy-start.3 = (bf16[9,1536]{1,0:T(8,128)(2,1)S(1)}, bf16[9,1536]{1,0:T(8,128)(2,1)}, u32[]{:S(2)}) copy-start(bf16[9,1536]{1,0:T(8,128)(2,1)} %taps_ref.1) | copy-start | bytes 82948
  70.4 33.5 %copy-start.4 = (s32[3]{0:T(128)S(1)}, s32[3]{0:T(128)}, u32[]{:S(2)}) copy-start(s32[3]{0:T(128)} %pad_add_fusion.place_ref) | copy-start | bytes 40
  131.6 7.8 %copy-start.5 = (bf16[16,112,128]{2,1,0:T(8,128)(2,1)}, bf16[16,112,128]{2,1,0:T(8,128)(2,1)S(1)}, u32[]{:S(2)}) copy-start(bf16[16,112,128]{2,1,0:T(8,128)(2,1)S(1)} %all_to_all.27.d_mixed_in) | copy-start | bytes 1376260
  132.3 18.1 %all-to-all-start.3 = ((f32[8,16,128]{2,1,0:T(8,128)}), f32[8,16,128]{2,1,0:T(8,128)S(1)}, u32[]{:S(2)}, u32[]{:S(2)}) async-start(f32[8,16,128]{2,1,0:T(8,128)} %broadcast_in_dim.16), calls=%async_computation.3 | async-start | bytes 131072 | tf_op jit(solution)/shard_map/small_sums/all_to_all | solution.py:502
  150.5 35.5 %all-to-all-start.4 = ((bf16[32,112,128]{2,1,0:T(8,128)(2,1)}), bf16[32,112,128]{2,1,0:T(8,128)(2,1)S(1)}, u32[]{:S(2)}, u32[]{:S(2)}) async-start(bf16[32,112,128]{2,1,0:T(8,128)(2,1)} %backward.1), calls=%async_computation.4 | async-start | bytes 1835008 | tf_op jit(solution)/shard_map/grad_exchange/all_to_all | solution.py:531
Sparse Core Ops, SparseCore 0:
  10.7 58.0 all-gather.4

commit v4 on v3

--- a/solution.py
+++ b/solution.py
@@ -115,23 +115,33 @@
         return carry
 
     wt = wt_ref[...]
-    for c, copy in enumerate(copies):
-        copy.wait()
-        rows = normed[c * per : (c + 1) * per].reshape(per * WIN, normed.shape[2])
+
+    def project(c, carry):
+        here = pl.ds(c * per, per)
+        pltpu.make_async_copy(gathered_ref.at[here], normed.at[here], sems.at[c]).wait()
+        rows = normed[here].reshape(per * WIN, normed.shape[2])
         part = dot(wt, rows, (1, 1))
-        at = slice(WIN + c * per * WIN, WIN + (c + 1) * per * WIN)
+        at = pl.ds(pl.multiple_of((1 + c * per) * WIN, WIN), per * WIN)
         qkvt_ref[:, at] = part.astype(BF16)
         k_ref[at, 0:hd] = part[hd : 2 * hd].T.astype(BF16)
         v_ref[at, :] = part[2 * hd :].T.astype(BF16)
-        final = c == len(copies) - 1
-        low, high = at.start - WIN * (c == 0), at.stop + WIN * final
-        done = pl.ds(low, high - low)
-        send(qkvt_ref.at[:, done], qkvt_out.at[:, done])
-        send(v_ref.at[done], v_out.at[done])
-        first, stop = max(c * per - 1, 0), (c + 1) * per - 1 + final
-        lax.fori_loop(first, stop, attend, 0, unroll=True)
-        done = pl.ds(first, stop - first)
-        send(soft_ref.at[done], soft_out.at[done])
+        return carry
+
+    lax.fori_loop(0, len(copies), project, 0)
+    send(qkvt_ref, qkvt_out)
+    send(v_ref, v_out)
+
+    def save(c):
+        here = pl.ds(c * per, per)
+        return pltpu.make_async_copy(soft_ref.at[here], soft_out.at[here], out_sems.at[2 + c])
+
+    def attend_group(c, carry):
+        for j in range(per):
+            attend(c * per + j, carry)
+        save(c).start()
+        return carry
+
+    lax.fori_loop(0, len(copies), attend_group, 0)
 
     def edges(i, carry):
         both = jnp.where(column < EDGE, mixed[i + 2], mixed[i]).T
@@ -140,7 +150,7 @@
         return carry
 
     lax.fori_loop(0, blocks, edges, 0, unroll=4)
-    for copy in sends:
+    for copy in sends + [save(c) for c in range(len(copies))]:
         copy.wait()
 
 
@@ -267,20 +277,28 @@
     blocks, width = gathered_ref.shape[0], gathered_ref.shape[2]
     hd = v_ref.shape[1]
     total = blocks * WIN
-    groups = sems.shape[0]
+    groups = sems.shape[0] - 1
     per = blocks // groups
-    copies = []
-    for c in range(groups):
-        low, high = (2 + c * per) * WIN * (c > 0), (2 + (c + 1) * per) * WIN
-        window, own = pl.ds(low, high - low), pl.ds(c * per, per)
-        copies.append([
+    lead = pl.ds(0, 2 * WIN)
+    ahead = [
+        pltpu.make_async_copy(v_in.at[lead], v_ref.at[lead], sems.at[groups, 0]),
+        pltpu.make_async_copy(qkvt_in.at[:, lead], qkvt_ref.at[:, lead], sems.at[groups, 1]),
+    ]
+
+    def group_copies(c):
+        window = pl.ds(pl.multiple_of((2 + c * per) * WIN, WIN), per * WIN)
+        own = pl.ds(c * per, per)
+        return [
             pltpu.make_async_copy(v_in.at[window], v_ref.at[window], sems.at[c, 0]),
             pltpu.make_async_copy(d_mixed_in.at[own], in_ref.at[own], sems.at[c, 1]),
             pltpu.make_async_copy(soft_in.at[own], soft_ref.at[own], sems.at[c, 2]),
             pltpu.make_async_copy(qkvt_in.at[:, window], qkvt_ref.at[:, window], sems.at[c, 3]),
-        ])
-    for group in copies:
-        for copy in group:
+        ]
+
+    for copy in ahead:
+        copy.start()
+    for c in range(groups):
+        for copy in group_copies(c):
             copy.start()
     steps = fetch_sems.shape[0]
     step = width // steps
@@ -311,13 +329,19 @@
         d_value[:, window] += dot(d_mixed, soft, (1, 1))
         return carry
 
-    for c, group in enumerate(copies):
-        for copy in group:
+    for fetch in fetches:
+        fetch.start()
+    for copy in ahead:
+        copy.wait()
+
+    def attend_group(c, carry):
+        for copy in group_copies(c):
             copy.wait()
-        if c == 0:
-            for fetch in fetches:
-                fetch.start()
-        lax.fori_loop(c * per, (c + 1) * per, attend, 0, unroll=True)
+        for j in range(per):
+            attend(c * per + j, carry)
+        return carry
+
+    lax.fori_loop(0, groups, attend_group, 0)
     joined[0:hd, :] = d_query[...]
     joined[hd : 2 * hd, :] = d_key[:, WIN : WIN + total].astype(BF16)
     joined[2 * hd :, :] = d_value[:, WIN : WIN + total].astype(BF16)
@@ -327,28 +351,35 @@
     third = share // (repeats - 1)
     lane = lax.broadcasted_iota(jnp.int32, (1, LANES), 1) // rest
     each = step // share
-    sends = []
-    for c, fetch in enumerate(fetches):
-        fetch.wait()
-        rows = normed[:, :, c * step : (c + 1) * step].reshape(total, step)
-        part = dot(joined[...], rows, (1, 0))
+
+    def send(c):
+        done = pl.ds(c * each, each)
+        return pltpu.make_async_copy(out_ref.at[done], message_out.at[done], out_sems.at[c])
+
+    def gradient(c, carry):
+        columns = pl.ds(pl.multiple_of(c * step, LANES), step)
+        pltpu.make_async_copy(
+            gathered_ref.at[:, :, columns], normed.at[:, :, columns], fetch_sems.at[c]
+        ).wait()
+        part = dot(joined[...], normed[:, :, columns].reshape(total, step), (1, 0))
         tail = part[2 * LANES :]
-        grad[c] = jnp.concatenate([part[: 2 * LANES]] + [tail] * repeats, axis=0).T
+        grad[...] = jnp.concatenate([part[: 2 * LANES]] + [tail] * repeats, axis=0).T
         for j in range(each):
             d = c * each + j
             at = slice(j * share, (j + 1) * share)
-            out_ref[d, 0:share, :] = grad[c, at, 0:LANES].astype(BF16)
-            out_ref[d, share : 2 * share, :] = grad[c, at, LANES : 2 * LANES].astype(BF16)
+            out_ref[d, 0:share, :] = grad[at, 0:LANES].astype(BF16)
+            out_ref[d, share : 2 * share, :] = grad[at, LANES : 2 * LANES].astype(BF16)
             packed = jnp.zeros((third, LANES), F32)
             for i in range(repeats - 1):
                 first = j * share + i * third
-                packed = jnp.where(lane == i, grad[c, first : first + third, 2 * LANES :], packed)
+                packed = jnp.where(lane == i, grad[first : first + third, 2 * LANES :], packed)
             out_ref[d, 2 * share :, :] = packed.astype(BF16)
-        done = pl.ds(c * each, each)
-        sends.append(pltpu.make_async_copy(out_ref.at[done], message_out.at[done], out_sems.at[c]))
-        sends[-1].start()
-    for send in sends:
-        send.wait()
+        send(c).start()
+        return carry
+
+    lax.fori_loop(0, steps, gradient, 0)
+    for c in range(steps):
+        send(c).wait()
 
 
 def sum_kernel(in_ref, grad_ref):
@@ -454,7 +485,7 @@
                 pltpu.VMEM((blocks, 3 * WIN, WIN), BF16),
                 pltpu.VMEM((3 * WIN, WIN), F32),
                 pltpu.SemaphoreType.DMA((4,)),
-                pltpu.SemaphoreType.DMA((12,)),
+                pltpu.SemaphoreType.DMA((6,)),
             ],
             compiler_params=params(54),
         )(lengths, gathered, wt)
@@ -514,13 +545,13 @@
                 pltpu.VMEM((hd, total + 2 * WIN), F32),
                 pltpu.VMEM((hd, total + 2 * WIN), F32),
                 pltpu.VMEM((3 * hd, total), BF16),
-                pltpu.VMEM((4, width // 4, 3 * LANES), F32),
+                pltpu.VMEM((width // 4, 3 * LANES), F32),
                 pltpu.VMEM((3 * hd, total + 2 * WIN), BF16),
                 pltpu.VMEM((total + 2 * WIN, hd), BF16),
                 pltpu.VMEM((blocks, 3 * WIN, WIN), BF16),
                 pltpu.VMEM((blocks, hd + small_rows, WIN), BF16),
                 pltpu.VMEM((shares, 2 * share + third, LANES), BF16),
-                pltpu.SemaphoreType.DMA((4, 4)),
+                pltpu.SemaphoreType.DMA((5, 4)),
                 pltpu.SemaphoreType.DMA((4,)),
                 pltpu.SemaphoreType.DMA((4,)),
             ],

time: 194 us -> 195 us (level)
  transfers between devices with their start and end apart: 9 -> 9, of which waited for: 3 -> 3; matrix products, arithmetic and copies ran while one was open for 1% -> 1% of each run, Pallas kernels for 12% -> 13%
where the time goes in v4:
time: 195 us
  blocking collectives  94.8 us (49%)
  starting transfers between devices  38 us (19%)
  Pallas kernels  36.3 us (19%)
  between operations  14.9 us (8%)
  waiting for transfers between devices  7.05 us (4%)
  other arithmetic  1.96 us (1%)
    all_to_all x1, blocking collectives, on_device(): columns = lax.all_to_all(columns, 'seq', 0, 0, axis_index_groups=same)  27.9 us
    all_to_all x1, blocking collectives, on_device(): mixed = lax.all_to_all(mixed, 'seq', 0, 0)  21 us
    all_to_all x1, blocking collectives, on_device(): d_mixed = lax.all_to_all(d_mixed, 'seq', 0, 0)  18.6 us
    all_gather x1, blocking collectives, on_device(): small = lax.all_gather(small, 'seq')  17.1 us
    pallas_call x1, Pallas kernels, on_device(): pl.pallas_call(forward_kernel, in_specs=[SMEM, HBM, VMEM], out_specs=[VME...  12.5 us
    pallas_call x1, Pallas kernels, on_device(): pl.pallas_call(functools.partial(backward_kernel, shares), in_specs=[HBM]...  11.3 us
    all_gather x1, blocking collectives, on_device(): lax.all_gather(small, 'dp', axis_index_groups=across)  10.2 us
    pallas_call x1, Pallas kernels, on_device(): pl.pallas_call(functools.partial(middle_kernel, total), in_specs=[SMEM] +...  8.86 us
  transfers between devices with their start and end apart: 9, of which 3 were waited for; matrix products, arithmetic and copies ran while one was open for 1% of the time, Pallas kernels for 13%

profile of v4, /device:TPU:1, one launch (start us, length us, event | category | flops | bytes accessed | tf_op | source)
XLA Modules:
  0.0 194.7 jit_solution(14316899270585122659)
XLA Ops:
  7.2 0.0 copy-start
  7.2 0.0 all-gather.5.cloned.1.call-start
  7.2 2.1 %norm.1 = bf16[128,1536]{1,0:T(8,128)(2,1)} custom-call(bf16[128,1536]{1,0:T(8,128)(2,1)} %bitcast.21), custom_call_target="tpu_custom_call" | custom-call | tf_op jit(solution)/shard_map/norm/pallas_call | solution.py:419
  9.4 0.0 all-gather.5.cloned.1.call-update
  9.4 0.0 copy-done
  9.4 0.1 broadcast_in_dim.14
  9.5 27.9 %all_to_all.25 = bf16[8,96,384]{2,1,0:T(8,128)(2,1)S(1)} all-to-all(bf16[8,96,384]{2,1,0:T(8,128)(2,1)S(1)} %broadcast_in_dim.14), channel_id=1, replica_groups={{0,2,4,6,8,10,12,14},{1,3,5,7,9,11,13,15},{16,18,20,22,24,26,28,30},{17..., dimensions={0} | all-to-all | bytes 1179648 | tf_op jit(solution)/shard_map/w_out_columns/all_to_all | solution.py:450
  37.4 0.0 copy-start.1
  37.4 0.0 copy-start.2
  37.4 0.0 copy-start.6
  37.4 6.4 %collective-permute-start = (bf16[8,96,384]{2,1,0:T(8,128)(2,1)S(1)}, bf16[8,96,384]{2,1,0:T(8,128)(2,1)S(1)}, u32[]{:S(2)}, u32[]{:S(2)}) collective-permute-start(bf16[8,96,384]{2,1,0:T(8,128)(2,1)S(1)} %all_to_all.25), channel_id=1, source_target_pairs={{0,1},{1,0},{2,3},{3,2},{4,5},{5,4},{6,7},{7,6},{8,9},{9,8},{10,11... | collective-permute-start | bytes 1769480 | tf_op jit(solution)/shard_map/w_out_columns/ppermute | solution.py:451
  43.8 0.1 constant_dynamic-update-slice_fusion.1
  43.9 1.5 collective-permute-done
  45.4 0.1 constant_dynamic-update-slice_fusion.own_ref
  45.5 4.4 %collective-permute-start.1 = (bf16[16,96,384]{2,1,0:T(8,128)(2,1)S(1)}, bf16[16,96,384]{2,1,0:T(8,128)(2,1)S(1)}, u32[]{:S(2)}, u32[]{:S(2)}) collective-permute-start(bf16[16,96,384]{2,1,0:T(8,128)(2,1)S(1)} %constant_dynamic-update-slice_fusion.own_ref), channel_id=1, source_target_pairs={{0,128},{1,385},{2,130},{3,387},{4,132},{5,389},{6,134},{7,391},{8... | collective-permute-start | bytes 3538952 | tf_op jit(solution)/shard_map/w_out_columns/ppermute | solution.py:457
  49.9 0.0 copy-done.1
  49.9 0.0 copy-done.2
  50.0 0.6 pad_maximum_fusion
  50.6 1.9 collective-permute-start.2
  52.5 0.6 pad_maximum_fusion.1
  53.1 2.4 %collective-permute-start.3 = (bf16[16,1536]{1,0:T(8,128)(2,1)}, bf16[16,1536]{1,0:T(8,128)(2,1)S(1)}, u32[]{:S(2)}, u32[]{:S(2)}) collective-permute-start(bf16[16,1536]{1,0:T(8,128)(2,1)} %pad_maximum_fusion.1), channel_id=1, source_target_pairs={{1,0},{2,1},{3,2},{4,3},{5,4},{6,5},{7,6},{8,7},{9,8},{10,9},{11,1... | collective-permute-start | bytes 147464 | tf_op jit(solution)/shard_map/halo/ppermute | solution.py:439
  56.2 0.7 pad_add_fusion.place_ref
  56.9 0.0 copy-done.6
  56.9 0.7 reshape.24.shift_ref
  57.6 0.0 collective-permute-done.2.prev_in
  57.6 2.4 %collective-permute-done.3.next_in = bf16[16,1536]{1,0:T(8,128)(2,1)S(1)} collective-permute-done((bf16[16,1536]{1,0:T(8,128)(2,1)}, bf16[16,1536]{1,0:T(8,128)(2,1)S(1)}, u32[]{:S(2)}, u32[]{:S(2)}) %collective-permute-start.3) | collective-permute-done | bytes 49184 | tf_op jit(solution)/shard_map/halo/ppermute | solution.py:439
  59.9 3.1 %collective-permute-done.1.near_ref = bf16[16,96,384]{2,1,0:T(8,128)(2,1)S(1)} collective-permute-done((bf16[16,96,384]{2,1,0:T(8,128)(2,1)S(1)}, bf16[16,96,384]{2,1,0:T(8,128)(2,1)S(1)}, u32[]{:S(2)}, u32[]{:S(2)}) %collective-permute-start.1) | collective-permute-done | bytes 1179680 | tf_op jit(solution)/shard_map/w_out_columns/ppermute | solution.py:457
  63.0 5.4 %collective-permute-start.5 = (bf16[16,96,384]{2,1,0:T(8,128)(2,1)S(1)}, bf16[16,96,384]{2,1,0:T(8,128)(2,1)}, u32[]{:S(2)}, u32[]{:S(2)}) collective-permute-start(bf16[16,96,384]{2,1,0:T(8,128)(2,1)S(1)} %collective-permute-done.1.near_ref), channel_id=1, source_target_pairs={{0,128},{1,385},{2,130},{3,387},{4,132},{5,389},{6,134},{7,391},{8... | collective-permute-start | bytes 3538952 | tf_op jit(solution)/shard_map/w_out_columns/ppermute | solution.py:464
  68.5 1.9 collective-permute-start.4
  70.4 0.0 all-gather.5.cloned.1.call-done
  70.4 0.0 copy-start.3
  70.4 0.0 copy-start.4
  70.4 12.5 %forward.1 = (bf16[16,112,128]{2,1,0:T(8,128)(2,1)}, bf16[288,2304]{1,0:T(8,128)(2,1)}, bf16[2304,96]{1,0:T(8,128)(2,1)}, bf16[16,384,128]{2,1,0:T(8,128)(2,1)}) custom-call(s32[1]{0:T(128)S(6)} %copy.14.len_ref, bf16[16,128,1536]{2,1,0:T(8,128)(2,1)} %bitcast.25, bf16[288,1536]{1,0:T(8,128)(2,1)} %bitcast.27), custom_call_target="tpu_custom_call" | custom-call | tf_op jit(solution)/shard_map/forward/pallas_call | solution.py:469
  82.9 0.0 collective-permute-done.5.far_ref
  82.9 0.0 collective-permute-done.4.twin_ref
  82.9 21.0 %all_to_all.26.mix_in = bf16[16,112,128]{2,1,0:T(8,128)(2,1)S(1)} all-to-all(bf16[16,112,128]{2,1,0:T(8,128)(2,1)} %get-tuple-element.31), channel_id=1, replica_groups=mesh['dp'=32,'seq'=16] {'seq'}, dimensions={0} | all-to-all | bytes 917504 | tf_op jit(solution)/shard_map/mixed_exchange/all_to_all | solution.py:494
  103.9 0.0 copy-done.3
  103.9 0.0 copy-done.4
  103.9 8.9 %middle.1 = (bf16[128,1536]{1,0:T(8,128)(2,1)}, bf16[16,112,128]{2,1,0:T(8,128)(2,1)S(1)}) custom-call(s32[3]{0:T(128)S(1)} %copy-done.4, bf16[16,112,128]{2,1,0:T(8,128)(2,1)S(1)} %all_to_all.26.mix_in, bf16[128,1536]{1,0:T(8,128)(2,1)S(1)} %bitcast.22, bf16[128,1536]{1,0:T(8,128)(2,1)S(1)} %bitcast.24, ...), custom_call_target="tpu_custom_call" | custom-call | tf_op jit(solution)/shard_map/middle/pallas_call | solution.py:497
  112.8 18.6 %all_to_all.27.d_mixed_in = bf16[16,112,128]{2,1,0:T(8,128)(2,1)S(1)} all-to-all(bf16[16,112,128]{2,1,0:T(8,128)(2,1)S(1)} %get-tuple-element.40), channel_id=1, replica_groups=mesh['dp'=32,'seq'=16] {'seq'}, dimensions={0} | all-to-all | bytes 917504 | tf_op jit(solution)/shard_map/d_mixed_exchange/all_to_all | solution.py:525
  131.4 0.0 copy-start.5
  131.5 0.7 broadcast_in_dim.16
  132.1 7.1 %all-to-all-start.3 = ((f32[8,16,128]{2,1,0:T(8,128)}), f32[8,16,128]{2,1,0:T(8,128)S(1)}, u32[]{:S(2)}, u32[]{:S(2)}) async-start(f32[8,16,128]{2,1,0:T(8,128)} %broadcast_in_dim.16), calls=%async_computation.3 | async-start | bytes 131072 | tf_op jit(solution)/shard_map/small_sums/all_to_all | solution.py:533
  139.2 0.0 copy-done.5
  139.2 11.3 %backward.1 = bf16[32,112,128]{2,1,0:T(8,128)(2,1)} custom-call(bf16[16,112,128]{2,1,0:T(8,128)(2,1)} %copy-done.5, bf16[16,128,1536]{2,1,0:T(8,128)(2,1)} %bitcast.26, bf16[288,2304]{1,0:T(8,128)(2,1)} %get-tuple-element.41.qkvt_in, bf16[2304,96]{1,0:T(8,128)(2,1)} %get-tuple-element.42.v_in, bf16[16,384,128]{2,1,0:T(8,128)(2,1)} %get-tuple-element.43.soft_in), custom_call_target="tpu_custom_call" | custom-call | tf_op jit(solution)/shard_map/backward/pallas_call | solution.py:537
  150.6 0.0 all-to-all-done.3
  150.6 8.5 %all-to-all-start.4 = ((bf16[32,112,128]{2,1,0:T(8,128)(2,1)}), bf16[32,112,128]{2,1,0:T(8,128)(2,1)S(1)}, u32[]{:S(2)}, u32[]{:S(2)}) async-start(bf16[32,112,128]{2,1,0:T(8,128)(2,1)} %backward.1), calls=%async_computation.4 | async-start | bytes 1835008 | tf_op jit(solution)/shard_map/grad_exchange/all_to_all | solution.py:562
  159.1 10.2 %all-gather.1 = f32[64,128]{1,0:T(8,128)S(1)} all-gather(f32[16,128]{1,0:T(8,128)S(1)} %reduce_sum.28), channel_id=3, replica_groups={{0,128,256,384},{16,144,272,400},{32,160,288,416},{48,176,304,432},{64,..., dimensions={0}, use_global_device_ids=true | all-gather | bytes 40960 | tf_op jit(solution)/shard_map/small_gathers/all_gather | solution.py:565
  169.3 17.1 %all-gather.2 = f32[256,128]{1,0:T(8,128)S(1)} all-gather(f32[16,128]{1,0:T(8,128)S(1)} %reduce_sum.29), channel_id=4, replica_groups=mesh['dp'=32,'seq'=16] {'seq'}, dimensions={0}, use_global_device_ids=true | all-gather | bytes 139264 | tf_op jit(solution)/shard_map/small_gathers/all_gather | solution.py:566
  186.4 0.7 spread.1
  187.1 0.0 all-to-all-done.4.in_ref
  187.1 0.8 sum.1
  (7 shorter events, 0.1 us)
Async XLA Ops:
  7.2 2.2 %copy-start = (bf16[1,96,1536]{2,1,0:T(8,128)(2,1)S(1)}, bf16[1,96,1536]{2,1,0:T(8,128)(2,1)}, u32[]{:S(2)}) copy-start(bf16[1,96,1536]{2,1,0:T(8,128)(2,1)} %param.11) | copy-start | bytes 884740
  7.2 63.2 %all-gather.5.cloned.1.call-start = ((), (), s32[]{:S(2)}) async-start(), calls=%async_computation.5 | async-start | bytes 6684672 | tf_op jit(solution)/shard_map/gather/all_gather | solution.py:432
  37.4 12.5 %copy-start.1 = (bf16[1,128,1536]{2,1,0:T(8,128)(2,1)S(1)}, bf16[1,128,1536]{2,1,0:T(8,128)(2,1)}, u32[]{:S(2)}) copy-start(bf16[1,128,1536]{2,1,0:T(8,128)(2,1)} %param.8) | copy-start | bytes 1179652
  37.4 12.5 %copy-start.2 = (bf16[1,128,1536]{2,1,0:T(8,128)(2,1)S(1)}, bf16[1,128,1536]{2,1,0:T(8,128)(2,1)}, u32[]{:S(2)}) copy-start(bf16[1,128,1536]{2,1,0:T(8,128)(2,1)} %param.15) | copy-start | bytes 1179652
  37.4 19.4 %copy-start.6 = (f32[1536]{0:T(1024)S(1)}, f32[1536]{0:T(1024)}, u32[]{:S(2)}) copy-start(f32[1536]{0:T(1024)} %param.13) | copy-start | bytes 18436
  37.4 8.0 %collective-permute-start = (bf16[8,96,384]{2,1,0:T(8,128)(2,1)S(1)}, bf16[8,96,384]{2,1,0:T(8,128)(2,1)S(1)}, u32[]{:S(2)}, u32[]{:S(2)}) collective-permute-start(bf16[8,96,384]{2,1,0:T(8,128)(2,1)S(1)} %all_to_all.25), channel_id=1, source_target_pairs={{0,1},{1,0},{2,3},{3,2},{4,5},{5,4},{6,7},{7,6},{8,9},{9,8},{10,11... | collective-permute-start | bytes 1769480 | tf_op jit(solution)/shard_map/w_out_columns/ppermute | solution.py:451
  45.5 17.5 %collective-permute-start.1 = (bf16[16,96,384]{2,1,0:T(8,128)(2,1)S(1)}, bf16[16,96,384]{2,1,0:T(8,128)(2,1)S(1)}, u32[]{:S(2)}, u32[]{:S(2)}) collective-permute-start(bf16[16,96,384]{2,1,0:T(8,128)(2,1)S(1)} %constant_dynamic-update-slice_fusion.own_ref), channel_id=1, source_target_pairs={{0,128},{1,385},{2,130},{3,387},{4,132},{5,389},{6,134},{7,391},{8... | collective-permute-start | bytes 3538952 | tf_op jit(solution)/shard_map/w_out_columns/ppermute | solution.py:457
  50.6 7.0 %collective-permute-start.2 = (bf16[16,1536]{1,0:T(8,128)(2,1)}, bf16[16,1536]{1,0:T(8,128)(2,1)S(1)}, u32[]{:S(2)}, u32[]{:S(2)}) collective-permute-start(bf16[16,1536]{1,0:T(8,128)(2,1)} %pad_maximum_fusion), channel_id=1, source_target_pairs={{0,1},{1,2},{2,3},{3,4},{4,5},{5,6},{6,7},{7,8},{8,9},{9,10},{10,1... | collective-permute-start | bytes 147464 | tf_op jit(solution)/shard_map/halo/ppermute | solution.py:438
  53.1 6.8 %collective-permute-start.3 = (bf16[16,1536]{1,0:T(8,128)(2,1)}, bf16[16,1536]{1,0:T(8,128)(2,1)S(1)}, u32[]{:S(2)}, u32[]{:S(2)}) collective-permute-start(bf16[16,1536]{1,0:T(8,128)(2,1)} %pad_maximum_fusion.1), channel_id=1, source_target_pairs={{1,0},{2,1},{3,2},{4,3},{5,4},{6,5},{7,6},{8,7},{9,8},{10,9},{11,1... | collective-permute-start | bytes 147464 | tf_op jit(solution)/shard_map/halo/ppermute | solution.py:439
  63.0 19.9 %collective-permute-start.5 = (bf16[16,96,384]{2,1,0:T(8,128)(2,1)S(1)}, bf16[16,96,384]{2,1,0:T(8,128)(2,1)}, u32[]{:S(2)}, u32[]{:S(2)}) collective-permute-start(bf16[16,96,384]{2,1,0:T(8,128)(2,1)S(1)} %collective-permute-done.1.near_ref), channel_id=1, source_target_pairs={{0,128},{1,385},{2,130},{3,387},{4,132},{5,389},{6,134},{7,391},{8... | collective-permute-start | bytes 3538952 | tf_op jit(solution)/shard_map/w_out_columns/ppermute | solution.py:464
  68.5 14.5 %collective-permute-start.4 = (bf16[16,96,384]{2,1,0:T(8,128)(2,1)S(1)}, bf16[16,96,384]{2,1,0:T(8,128)(2,1)}, u32[]{:S(2)}, u32[]{:S(2)}) collective-permute-start(bf16[16,96,384]{2,1,0:T(8,128)(2,1)S(1)} %collective-permute-done.1.near_ref), channel_id=1, source_target_pairs={{0,1},{1,0},{2,3},{3,2},{4,5},{5,4},{6,7},{7,6},{8,9},{9,8},{10,11... | collective-permute-start | bytes 3538952 | tf_op jit(solution)/shard_map/w_out_columns/ppermute | solution.py:463
  70.4 33.5 %copy-start.3 = (bf16[9,1536]{1,0:T(8,128)(2,1)S(1)}, bf16[9,1536]{1,0:T(8,128)(2,1)}, u32[]{:S(2)}) copy-start(bf16[9,1536]{1,0:T(8,128)(2,1)} %taps_ref.1) | copy-start | bytes 82948
  70.4 33.5 %copy-start.4 = (s32[3]{0:T(128)S(1)}, s32[3]{0:T(128)}, u32[]{:S(2)}) copy-start(s32[3]{0:T(128)} %pad_add_fusion.place_ref) | copy-start | bytes 40
  131.4 7.8 %copy-start.5 = (bf16[16,112,128]{2,1,0:T(8,128)(2,1)}, bf16[16,112,128]{2,1,0:T(8,128)(2,1)S(1)}, u32[]{:S(2)}) copy-start(bf16[16,112,128]{2,1,0:T(8,128)(2,1)S(1)} %all_to_all.27.d_mixed_in) | copy-start | bytes 1376260
  132.1 18.4 %all-to-all-start.3 = ((f32[8,16,128]{2,1,0:T(8,128)}), f32[8,16,128]{2,1,0:T(8,128)S(1)}, u32[]{:S(2)}, u32[]{:S(2)}) async-start(f32[8,16,128]{2,1,0:T(8,128)} %broadcast_in_dim.16), calls=%async_computation.3 | async-start | bytes 131072 | tf_op jit(solution)/shard_map/small_sums/all_to_all | solution.py:533
  150.6 36.5 %all-to-all-start.4 = ((bf16[32,112,128]{2,1,0:T(8,128)(2,1)}), bf16[32,112,128]{2,1,0:T(8,128)(2,1)S(1)}, u32[]{:S(2)}, u32[]{:S(2)}) async-start(bf16[32,112,128]{2,1,0:T(8,128)(2,1)} %backward.1), calls=%async_computation.4 | async-start | bytes 1835008 | tf_op jit(solution)/shard_map/grad_exchange/all_to_all | solution.py:562
Sparse Core Ops, SparseCore 0:
  10.7 58.0 all-gather.4
